TPU v7x, 32 devices: a whole 2x2x4 slice. The times are simulated.
32 devices in a mesh: expert: 4 (over y, x), ctx: 2 (over core), dp: 4 (over z).
Axes of the slice: x: 2, y: 2, z: 4, core: 2. Of those that a mesh axis runs over, the one named last changes fastest.
Arguments:
- prompt_tokens: bfloat16 [4, 1024, 2048], P('dp', 'ctx'), may hold values from -6 to 6
- sequel_tokens: bfloat16 [4, 2, 512, 2048], P('dp', None, 'ctx'), may hold values from -6 to 6
- attention_gain: float32 [2048], replicated, may hold values from 0.1 to 1.9
- query_weight: bfloat16 [2048, 4096], P(None, 'expert'), may hold values from -0.125 to 0.125
- key_weight: bfloat16 [2048, 512], replicated, may hold values from -0.125 to 0.125
- value_weight: bfloat16 [2048, 512], replicated, may hold values from -0.125 to 0.125
- query_gain: float32 [128], replicated, may hold values from 0.1 to 1.9
- key_gain: float32 [128], replicated, may hold values from 0.1 to 1.9
- out_weight: bfloat16 [4096, 2048], P('expert'), may hold values from -1.5 to 1.5
- feed_gain: float32 [2048], replicated, may hold values from 0.1 to 1.9
- router_weight: bfloat16 [2048, 16], replicated, may hold values from -0.0625 to 0.0625
- gate_up_weight: bfloat16 [16, 2048, 1536], P(('expert', 'dp')), may hold values from -0.125 to 0.125
- down_weight: bfloat16 [16, 768, 2048], P(('expert', 'dp')), may hold values from -0.875 to 0.875
- prompt_routes: int32 [4, 1024, 8], P('dp', 'ctx'), may hold values from 0 to 15, all different within a row; in each aligned block of 128 rows (0 to 127, 128 to 255, ..., all dimensions but the last counted through in order) at most 128 rows name the same one
- sequel_routes: int32 [4, 2, 512, 8], P('dp', None, 'ctx'), may hold values from 0 to 15, all different within a row; in each aligned block of 64 rows (0 to 63, 64 to 127, ..., all dimensions but the last counted through in order) at most 64 rows name the same one
- prompt_cotangent: bfloat16 [4, 1024, 2048], P('dp', 'ctx'), may hold values from -6 to 6
- sequel_cotangent: bfloat16 [4, 2, 512, 2048], P('dp', None, 'ctx'), may hold values from -6 to 6
Outputs:
- layer_prompt: bfloat16 [4, 1024, 2048], P('dp', 'ctx')
- layer_sequel: bfloat16 [4, 2, 512, 2048], P('dp', None, 'ctx')
- grad_prompt: bfloat16 [4, 1024, 2048], P('dp', 'ctx')
- grad_sequel: bfloat16 [4, 2, 512, 2048], P('dp', None, 'ctx')
- grad_attention_gain: float32 [2048], replicated
- grad_query: float32 [2048, 4096], P(None, 'expert')
- grad_key: float32 [2048, 512], replicated
- grad_value: float32 [2048, 512], replicated
- grad_query_gain: float32 [128], replicated
- grad_key_gain: float32 [128], replicated
- grad_out: float32 [4096, 2048], P('expert')
- grad_feed_gain: float32 [2048], replicated
- grad_router: float32 [2048, 16], replicated
- grad_gate_up: float32 [16, 2048, 1536], P(('expert', 'dp'))
- grad_down: float32 [16, 768, 2048], P(('expert', 'dp'))
Inputs may be any that keep to these rules, and one draw needn't show every extreme that they name: `prompt_routes`: each row names 8 different experts. In each aligned block of 128 rows (all leading dimensions together, in order) no expert is named by more than 128 rows, and in some block one expert is named by exactly 128 rows. `sequel_routes`: each row names 8 different experts. In each aligned block of 64 rows (all leading dimensions together, in order) no expert is named by more than 64 rows, and in some block one expert is named by exactly 64 rows.
All inputs are finite; a program needn't handle non-finite values.
Results may differ from a plain program's by a relative error of at most 0.028.
Values may be sent and summed in bfloat16 or wider, within the bound.
No kernel may reach another device: no remote copies, remote signals or barrier semaphores. Data moves between devices by JAX's collectives and lax.ppermute only.
A program may use at most 512 MiB of HBM per device.

v0:
```python
import math

import jax
import jax.numpy as jnp
from jax import lax
from jax.sharding import PartitionSpec as P

H = 32
KV = 4
P_SIZE = 1024


NORM_EPS = 1e-06
ROPE_BASE = 1000000.0
NEGATIVE_FILL = -1e30
HIGHEST = lax.Precision.HIGHEST


def rms_scaled(values, gain_row):
    return (
        values * lax.rsqrt(jnp.mean(values * values, axis=-1, keepdims=True) + NORM_EPS) * gain_row
    )


def rms_backward(values, gain_row, upstream):
    inverse = lax.rsqrt(jnp.mean(values * values, axis=-1, keepdims=True) + NORM_EPS)
    unit_rows = values * inverse
    scaled = upstream * gain_row
    inner_mean = jnp.mean(scaled * unit_rows, axis=-1, keepdims=True)
    return (inverse * (scaled - unit_rows * inner_mean), upstream * unit_rows)


def rotary_tables(positions, head_width):
    halfway = head_width // 2
    frequency = jnp.exp(
        jnp.arange(halfway, dtype=jnp.float32) * (-2.0 * math.log(ROPE_BASE) / head_width)
    )
    angles = positions[:, None] * frequency[None, :]
    return (jnp.cos(angles), jnp.sin(angles))


def rotate(values, cosine, sine_table):
    halfway = values.shape[-1] // 2
    first_half = values[..., :halfway]
    second_half = values[..., halfway:]
    cos_rows = cosine[:, None, :]
    sin_rows = sine_table[:, None, :]
    return jnp.concatenate(
        [
            first_half * cos_rows - second_half * sin_rows,
            second_half * cos_rows + first_half * sin_rows,
        ],
        axis=-1,
    )


def places(row_count, first_row, prompt_rows, sequel_rows):
    index_row = first_row + jnp.arange(row_count, dtype=jnp.int32)
    per_device = prompt_rows + 2 * sequel_rows
    owner_index = index_row // per_device
    inner_row = index_row % per_device
    in_sequel = inner_row >= prompt_rows
    offset = inner_row - prompt_rows
    segment = jnp.where(in_sequel, offset // sequel_rows + 1, 0)
    position = jnp.where(
        in_sequel,
        P_SIZE + owner_index * sequel_rows + offset % sequel_rows,
        owner_index * prompt_rows + inner_row,
    )
    return (segment, position)


def to_slices(whole, prompt_rows, sequel_rows, expert_parts):
    tail = whole.shape[1:]
    first_part = whole[:prompt_rows].reshape((expert_parts, prompt_rows // expert_parts) + tail)
    second_part = whole[prompt_rows : prompt_rows + sequel_rows].reshape(
        (expert_parts, sequel_rows // expert_parts) + tail
    )
    third_part = whole[prompt_rows + sequel_rows :].reshape(
        (expert_parts, sequel_rows // expert_parts) + tail
    )
    return jnp.concatenate([first_part, second_part, third_part], axis=1).reshape(whole.shape)


def from_slices(sorted_rows, prompt_rows, sequel_rows, expert_parts):
    tail = sorted_rows.shape[1:]
    share_rows = (prompt_rows + 2 * sequel_rows) // expert_parts
    lattice = sorted_rows.reshape((expert_parts, share_rows) + tail)
    prompt_share = prompt_rows // expert_parts
    sequel_share = sequel_rows // expert_parts
    first_part = lattice[:, :prompt_share].reshape((prompt_rows,) + tail)
    second_part = lattice[:, prompt_share : prompt_share + sequel_share].reshape(
        (sequel_rows,) + tail
    )
    third_part = lattice[:, prompt_share + sequel_share :].reshape((sequel_rows,) + tail)
    return jnp.concatenate([first_part, second_part, third_part], axis=0)


def capacity(prompt_rows, sequel_rows, expert_parts, experts, choices_per_token):
    prompt_block = prompt_rows // expert_parts
    sequel_block = sequel_rows // expert_parts
    most_prompt = max(2, min(prompt_block, 2 * prompt_block * choices_per_token // experts))
    most_sequel = max(2, min(sequel_block, 2 * sequel_block * choices_per_token // experts))
    return most_prompt + 2 * most_sequel


def move_slots(slot_rows):
    return lax.all_to_all(slot_rows, ("expert", "dp"), split_axis=0, concat_axis=0, tiled=True)


def on_device(
    prompt_tokens,
    sequel_tokens,
    attention_gain,
    query_weight,
    key_weight,
    value_weight,
    query_gain,
    key_gain,
    out_weight,
    feed_gain,
    router_weight,
    gate_up_weight,
    down_weight,
    prompt_routes,
    sequel_routes,
    prompt_cotangent,
    sequel_cotangent,
):
    expert_parts = lax.axis_size("expert")
    expert_index = lax.axis_index("expert")
    ctx_index = lax.axis_index("ctx")
    prompt_rows = prompt_tokens.shape[1]
    sequel_rows = sequel_tokens.shape[2]
    per_device = prompt_rows + 2 * sequel_rows
    share_rows = per_device // expert_parts
    model_width = prompt_tokens.shape[2]
    head_dim = query_gain.shape[0]
    query_heads = query_weight.shape[1] // head_dim
    group_size = H // KV
    kv_heads = max(1, query_heads // group_size)
    per_kv = query_heads // kv_heads
    kv_first = expert_index * query_heads // group_size
    kv_width = key_weight.shape[1]
    column_width = kv_width // expert_parts
    column_first = expert_index * column_width
    experts = router_weight.shape[1]
    choices_per_token = prompt_routes.shape[2]
    slot_count = capacity(prompt_rows, sequel_rows, expert_parts, experts, choices_per_token)
    local_experts = gate_up_weight.shape[0]
    hidden_units = down_weight.shape[1]
    score_scale = 1.0 / math.sqrt(head_dim)
    tokens = jnp.concatenate(
        [prompt_tokens[0], sequel_tokens[0, 0], sequel_tokens[0, 1]], axis=0
    ).astype(jnp.float32)
    hidden = rms_scaled(tokens, attention_gain).astype(jnp.bfloat16)
    key_mine = lax.dynamic_slice_in_dim(key_weight, kv_first * head_dim, kv_heads * head_dim, 1)
    value_mine = lax.dynamic_slice_in_dim(value_weight, kv_first * head_dim, kv_heads * head_dim, 1)
    query_pre = jnp.dot(hidden, query_weight, preferred_element_type=jnp.float32).reshape(
        per_device, query_heads, head_dim
    )
    key_pre = jnp.dot(hidden, key_mine, preferred_element_type=jnp.float32).reshape(
        per_device, kv_heads, head_dim
    )
    value_local = jnp.dot(hidden, value_mine, preferred_element_type=jnp.float32).astype(
        jnp.bfloat16
    )
    query_segment, query_position = places(
        per_device, ctx_index * per_device, prompt_rows, sequel_rows
    )
    cosine, sine_table = rotary_tables(query_position.astype(jnp.float32), head_dim)
    queries = rotate(rms_scaled(query_pre, query_gain), cosine, sine_table).astype(jnp.bfloat16)
    key_local = (
        rotate(rms_scaled(key_pre, key_gain), cosine, sine_table)
        .astype(jnp.bfloat16)
        .reshape(per_device, kv_heads * head_dim)
    )
    grouped = queries.reshape(per_device, kv_heads, per_kv, head_dim)

    def masked_scores(key_rows, first_row):
        key_segment, key_position = places(key_rows.shape[0], first_row, prompt_rows, sequel_rows)
        allowed = (key_position[None, :] <= query_position[:, None]) & (
            (key_segment[None, :] == 0) | (key_segment[None, :] == query_segment[:, None])
        )
        raw_scores = (
            jnp.einsum(
                "qkgd,tkd->kgqt",
                grouped,
                key_rows.reshape(-1, kv_heads, head_dim),
                preferred_element_type=jnp.float32,
            )
            * score_scale
        )
        return (jnp.where(allowed[None, None], raw_scores, NEGATIVE_FILL), allowed)

    peak_score = jnp.full((kv_heads, per_kv, per_device), NEGATIVE_FILL, jnp.float32)
    scores, allowed = masked_scores(
        lax.all_gather(key_local, "ctx", axis=0, tiled=True), jnp.int32(0)
    )
    new_peak = jnp.maximum(peak_score, jnp.max(scores, axis=-1))
    exp_scores = jnp.where(allowed[None, None], jnp.exp(scores - new_peak[..., None]), 0.0)
    total_weight = jnp.sum(exp_scores, axis=-1)
    log_total = new_peak + jnp.log(total_weight)
    key_rows = lax.all_gather(key_local, "ctx", axis=0, tiled=True)
    value_rows = lax.all_gather(value_local, "ctx", axis=0, tiled=True)
    scores, allowed = masked_scores(key_rows, jnp.int32(0))
    probs_low = jnp.where(allowed[None, None], jnp.exp(scores - log_total[..., None]), 0.0).astype(
        jnp.bfloat16
    )
    heads_exact = jnp.einsum(
        "kgqt,tkd->kgqd",
        probs_low,
        value_rows.reshape(-1, kv_heads, head_dim),
        preferred_element_type=jnp.float32,
    )
    heads_flat = (
        heads_exact.transpose(2, 0, 1, 3)
        .reshape(per_device, query_heads * head_dim)
        .astype(jnp.bfloat16)
    )
    heads_sorted = to_slices(heads_flat, prompt_rows, sequel_rows, expert_parts)
    attention_share = lax.psum_scatter(
        jnp.dot(heads_sorted, out_weight, preferred_element_type=jnp.float32).astype(jnp.bfloat16),
        "expert",
        scatter_dimension=0,
        tiled=True,
    ).astype(jnp.float32)
    tokens_mine = lax.dynamic_slice_in_dim(
        to_slices(tokens, prompt_rows, sequel_rows, expert_parts),
        expert_index * share_rows,
        share_rows,
        0,
    )
    residual = tokens_mine + attention_share
    normed = rms_scaled(residual, feed_gain).astype(jnp.bfloat16)
    logits = jnp.dot(normed, router_weight, preferred_element_type=jnp.float32)
    routes_all = jnp.concatenate(
        [prompt_routes[0], sequel_routes[0, 0], sequel_routes[0, 1]], axis=0
    )
    routes_mine = lax.dynamic_slice_in_dim(
        to_slices(routes_all, prompt_rows, sequel_rows, expert_parts),
        expert_index * share_rows,
        share_rows,
        0,
    )
    chosen_mask = (
        routes_mine[:, :, None] == jnp.arange(experts, dtype=jnp.int32)[None, None, :]
    ).astype(jnp.float32)
    chosen = jnp.sum(chosen_mask * logits[:, None, :], axis=-1)
    gate_weights = jax.nn.softmax(chosen, axis=-1)
    flat_routes = routes_mine.reshape(-1)
    flat_mask = chosen_mask.reshape(-1, experts).astype(jnp.int32)
    before = jnp.cumsum(flat_mask, axis=0) - flat_mask
    slot_rank = jnp.sum(before * flat_mask, axis=1)
    empty_slots = jnp.zeros((experts, slot_count, model_width), jnp.bfloat16)
    send_slots = empty_slots.at[flat_routes, slot_rank].set(
        jnp.repeat(normed, choices_per_token, axis=0)
    )
    arrived = move_slots(send_slots)
    source_rows = arrived.reshape(-1, local_experts, slot_count, model_width)
    gate_pre = jnp.einsum(
        "sjcd,jdf->sjcf", source_rows, gate_up_weight, preferred_element_type=jnp.float32
    )
    gate_part = gate_pre[..., :hidden_units]
    up_part = gate_pre[..., hidden_units:]
    active = (jax.nn.silu(gate_part) * up_part).astype(jnp.bfloat16)
    produced = jnp.einsum(
        "sjcf,jfd->sjcd", active, down_weight, preferred_element_type=jnp.float32
    ).astype(jnp.bfloat16)
    returned = move_slots(produced.reshape(arrived.shape))
    picked = (
        returned[flat_routes, slot_rank]
        .reshape(share_rows, choices_per_token, model_width)
        .astype(jnp.float32)
    )
    mixture = jnp.sum(gate_weights[..., None] * picked, axis=1)
    layer_share = (residual + mixture).astype(jnp.bfloat16)
    cotangent_all = jnp.concatenate(
        [prompt_cotangent[0], sequel_cotangent[0, 0], sequel_cotangent[0, 1]], axis=0
    ).astype(jnp.float32)
    upstream = lax.dynamic_slice_in_dim(
        to_slices(cotangent_all, prompt_rows, sequel_rows, expert_parts),
        expert_index * share_rows,
        share_rows,
        0,
    )
    slot_grads = (
        (gate_weights[..., None] * upstream[:, None, :])
        .reshape(-1, model_width)
        .astype(jnp.bfloat16)
    )
    gate_grads = jnp.sum(picked * upstream[:, None, :], axis=-1)
    grad_arrived = move_slots(empty_slots.at[flat_routes, slot_rank].set(slot_grads)).reshape(
        -1, local_experts, slot_count, model_width
    )
    active_grad = jnp.einsum(
        "sjcd,jfd->sjcf", grad_arrived, down_weight, preferred_element_type=jnp.float32
    )
    down_grad = jnp.einsum(
        "sjcf,sjcd->jfd", active, grad_arrived, preferred_element_type=jnp.float32
    )
    sigmoid_gate = jax.nn.sigmoid(gate_part)
    gate_side = active_grad * up_part * sigmoid_gate * (1.0 + gate_part * (1.0 - sigmoid_gate))
    up_side = active_grad * gate_part * sigmoid_gate
    pre_grad = jnp.concatenate([gate_side, up_side], axis=-1).astype(jnp.bfloat16)
    gate_up_grad = jnp.einsum(
        "sjcd,sjcf->jdf", source_rows, pre_grad, preferred_element_type=jnp.float32
    )
    row_grads = jnp.einsum(
        "sjcf,jdf->sjcd", pre_grad, gate_up_weight, preferred_element_type=jnp.float32
    ).astype(jnp.bfloat16)
    row_back = move_slots(row_grads.reshape(arrived.shape))
    normed_grad = jnp.sum(
        row_back[flat_routes, slot_rank]
        .reshape(share_rows, choices_per_token, model_width)
        .astype(jnp.float32),
        axis=1,
    )
    chosen_grad = gate_weights * (
        gate_grads - jnp.sum(gate_weights * gate_grads, axis=-1, keepdims=True)
    )
    logit_grad = jnp.sum(chosen_grad[..., None] * chosen_mask, axis=1)
    router_float = router_weight.astype(jnp.float32)
    normed_grad = normed_grad + jnp.dot(logit_grad, router_float.T, precision=HIGHEST)
    router_grad = jnp.dot(normed.astype(jnp.float32).T, logit_grad, precision=HIGHEST)
    residual_part, feed_terms = rms_backward(residual, feed_gain, normed_grad)
    residual_grad = upstream + residual_part
    feed_gain_grad = jnp.sum(feed_terms, axis=0)
    layer_sorted, grad_sorted = (
        lax.all_gather(
            layer_share.astype(jnp.float32).astype(jnp.bfloat16), "expert", axis=0, tiled=True
        ).astype(jnp.float32),
        lax.all_gather(residual_grad.astype(jnp.bfloat16), "expert", axis=0, tiled=True).astype(
            residual_grad.dtype
        ),
    )
    layer_full = from_slices(layer_sorted, prompt_rows, sequel_rows, expert_parts).astype(
        jnp.bfloat16
    )
    residual_low = grad_sorted.astype(jnp.bfloat16)
    out_weight_grad = lax.dot_general(
        heads_sorted, residual_low, (((0,), (0,)), ((), ())), preferred_element_type=jnp.float32
    )
    heads_grad_sorted = lax.dot_general(
        residual_low, out_weight, (((1,), (1,)), ((), ())), preferred_element_type=jnp.float32
    ).astype(jnp.bfloat16)
    heads_grad = from_slices(heads_grad_sorted, prompt_rows, sequel_rows, expert_parts).reshape(
        per_device, kv_heads, per_kv, head_dim
    )
    key_back, value_back = (
        lax.all_gather(key_local, "ctx", axis=0, tiled=True),
        lax.all_gather(value_local, "ctx", axis=0, tiled=True),
    )
    scores, allowed = masked_scores(key_back, 0)
    probabilities = jnp.where(allowed[None, None], jnp.exp(scores - log_total[..., None]), 0.0)
    back_keys = key_back.reshape(-1, kv_heads, head_dim)
    back_values = value_back.reshape(-1, kv_heads, head_dim)
    value_grads = jnp.einsum(
        "kgqt,qkgd->tkd",
        probabilities.astype(jnp.bfloat16),
        heads_grad,
        preferred_element_type=jnp.float32,
    )
    prob_grads = jnp.einsum(
        "qkgd,tkd->kgqt", heads_grad, back_values, preferred_element_type=jnp.float32
    )
    delta_rows = jnp.sum(probabilities * prob_grads, axis=-1)
    score_grads = (probabilities * (prob_grads - delta_rows[..., None])).astype(jnp.bfloat16)
    query_grads = (
        jnp.einsum("kgqt,tkd->qkgd", score_grads, back_keys, preferred_element_type=jnp.float32)
        * score_scale
    )
    key_grads = (
        jnp.einsum("kgqt,qkgd->tkd", score_grads, grouped, preferred_element_type=jnp.float32)
        * score_scale
    )
    key_sum, value_sum = (
        lax.psum_scatter(
            key_grads.reshape(-1, kv_heads * head_dim).astype(jnp.bfloat16),
            "ctx",
            scatter_dimension=0,
            tiled=True,
        ).astype(jnp.float32),
        lax.psum_scatter(
            value_grads.reshape(-1, kv_heads * head_dim).astype(jnp.bfloat16),
            "ctx",
            scatter_dimension=0,
            tiled=True,
        ).astype(jnp.float32),
    )
    key_turned = rotate(key_sum.reshape(per_device, kv_heads, head_dim), cosine, -sine_table)
    key_pre_grad, key_terms = rms_backward(key_pre, key_gain, key_turned)
    key_gain_grad = jnp.sum(key_terms, axis=(0, 1))
    query_turned = rotate(
        query_grads.reshape(per_device, query_heads, head_dim), cosine, -sine_table
    )
    query_pre_grad, query_terms = rms_backward(query_pre, query_gain, query_turned)
    query_gain_grad = jnp.sum(query_terms, axis=(0, 1))
    query_low = query_pre_grad.reshape(per_device, query_heads * head_dim).astype(jnp.bfloat16)
    kv_zeros = jnp.zeros((per_device, kv_width), jnp.float32)
    key_place = lax.dynamic_update_slice_in_dim(
        kv_zeros, key_pre_grad.reshape(per_device, kv_heads * head_dim), kv_first * head_dim, 1
    )
    value_place = lax.dynamic_update_slice_in_dim(kv_zeros, value_sum, kv_first * head_dim, 1)
    key_cols, value_cols = (
        lax.psum(key_place.astype(jnp.bfloat16), "expert").astype(jnp.float32),
        lax.psum(value_place.astype(jnp.bfloat16), "expert").astype(jnp.float32),
    )
    key_low = key_cols.astype(jnp.bfloat16)
    value_low = value_cols.astype(jnp.bfloat16)
    contract_rows = (((0,), (0,)), ((), ()))
    contract_cols = (((1,), (1,)), ((), ()))
    query_weight_grad = lax.dot_general(
        hidden, query_low, contract_rows, preferred_element_type=jnp.float32
    )
    key_weight_grad = lax.dot_general(
        hidden, key_low, contract_rows, preferred_element_type=jnp.float32
    )
    value_weight_grad = lax.dot_general(
        hidden, value_low, contract_rows, preferred_element_type=jnp.float32
    )
    key_block = lax.dynamic_slice_in_dim(key_low, column_first, column_width, 1)
    value_block = lax.dynamic_slice_in_dim(value_low, column_first, column_width, 1)
    key_weight_block = lax.dynamic_slice_in_dim(key_weight, column_first, column_width, 1)
    value_weight_block = lax.dynamic_slice_in_dim(value_weight, column_first, column_width, 1)
    hidden_grad = lax.dot_general(
        query_low, query_weight, contract_cols, preferred_element_type=jnp.float32
    )
    hidden_grad = hidden_grad + lax.dot_general(
        key_block, key_weight_block, contract_cols, preferred_element_type=jnp.float32
    )
    hidden_grad = hidden_grad + lax.dot_general(
        value_block, value_weight_block, contract_cols, preferred_element_type=jnp.float32
    )
    input_part, attention_terms = rms_backward(tokens, attention_gain, hidden_grad)
    attention_gain_grad = jnp.sum(attention_terms, axis=0)
    summed = (
        lax.psum(input_part.astype(jnp.bfloat16), "expert").astype(jnp.float32),
        lax.psum(attention_gain_grad.astype(jnp.bfloat16), "expert").astype(jnp.float32),
        lax.psum(feed_gain_grad.astype(jnp.bfloat16), "expert").astype(jnp.float32),
        lax.psum(query_gain_grad.astype(jnp.bfloat16), "expert").astype(jnp.float32),
        lax.psum(key_gain_grad.astype(jnp.bfloat16), "expert").astype(jnp.float32),
        lax.psum(router_grad.astype(jnp.bfloat16), "expert").astype(jnp.float32),
    )
    input_grad = (
        from_slices(grad_sorted, prompt_rows, sequel_rows, expert_parts) + summed[0]
    ).astype(jnp.bfloat16)
    totals = (
        lax.psum(query_weight_grad.astype(jnp.bfloat16), ("ctx", "dp")).astype(jnp.float32),
        lax.psum(out_weight_grad.astype(jnp.bfloat16), ("ctx", "dp")).astype(jnp.float32),
        lax.psum(key_weight_grad.astype(jnp.bfloat16), ("ctx", "dp")).astype(jnp.float32),
        lax.psum(value_weight_grad.astype(jnp.bfloat16), ("ctx", "dp")).astype(jnp.float32),
        lax.psum(summed[1].astype(jnp.bfloat16), ("ctx", "dp")).astype(jnp.float32),
        lax.psum(summed[2].astype(jnp.bfloat16), ("ctx", "dp")).astype(jnp.float32),
        lax.psum(summed[3].astype(jnp.bfloat16), ("ctx", "dp")).astype(jnp.float32),
        lax.psum(summed[4].astype(jnp.bfloat16), ("ctx", "dp")).astype(jnp.float32),
        lax.psum(summed[5].astype(jnp.bfloat16), ("ctx", "dp")).astype(jnp.float32),
    )
    expert_totals = (
        lax.psum(gate_up_grad.astype(jnp.bfloat16), "ctx").astype(jnp.float32),
        lax.psum(down_grad.astype(jnp.bfloat16), "ctx").astype(jnp.float32),
    )
    layer_prompt = layer_full[:prompt_rows][None]
    layer_sequel = layer_full[prompt_rows:].reshape(1, 2, sequel_rows, model_width)
    grad_prompt = input_grad[:prompt_rows][None]
    grad_sequel = input_grad[prompt_rows:].reshape(1, 2, sequel_rows, model_width)
    return (
        layer_prompt,
        layer_sequel,
        grad_prompt,
        grad_sequel,
        totals[4],
        totals[0],
        totals[2],
        totals[3],
        totals[6],
        totals[7],
        totals[1],
        totals[5],
        totals[8],
        expert_totals[0],
        expert_totals[1],
    )


def solution(mesh):
    placed = (
        P("dp", "ctx", None),
        P("dp", None, "ctx", None),
        P(),
        P(None, "expert"),
        P(),
        P(),
        P(),
        P(),
        P("expert", None),
        P(),
        P(),
        P(("expert", "dp"), None, None),
        P(("expert", "dp"), None, None),
        P("dp", "ctx", None),
        P("dp", None, "ctx", None),
        P("dp", "ctx", None),
        P("dp", None, "ctx", None),
    )
    return jax.shard_map(
        on_device,
        mesh=mesh,
        in_specs=placed,
        out_specs=(
            P("dp", "ctx", None),
            P("dp", None, "ctx", None),
            P("dp", "ctx", None),
            P("dp", None, "ctx", None),
            P(),
            P(None, "expert"),
            P(),
            P(),
            P(),
            P(),
            P("expert", None),
            P(),
            P(),
            P(("expert", "dp"), None, None),
            P(("expert", "dp"), None, None),
        ),
        check_vma=False,
    )
```

profile of v0, /device:TPU:0, one launch (start us, length us, event | category | flops | bytes accessed | tf_op | source)
XLA Modules:
  0.0 2761.5 jit_solution(2191098610917210169)
XLA Ops:
  43.7 23.8 fusion.3
  67.5 22.4 select_reduce_fusion
  96.0 26.4 convert_bitcast_fusion
  166.6 34.2 %reduce-scatter.4.cloned.1.call-done = bf16[256,2048]{1,0:T(8,128)(2,1)} async-done(((bf16[1024,2048]{1,0:T(8,128)(2,1)}), bf16[256,2048]{1,0:T(8,128)(2,1)}) %reduce-scatter.4.cloned.1.call-update) | async-done | bytes 1048592 | tf_op jit(solution)/shard_map/reduce_scatter | solution.py:222
  245.3 22.6 scatter_custom_fusion.1
  267.9 355.0 %all-to-all-done = bf16[16,256,2048]{2,1,0:T(8,128)(2,1)} async-done(((bf16[16,256,2048]{2,1,0:T(8,128)(2,1)}), bf16[16,256,2048]{2,1,0:T(8,128)(2,1)}, u32[]{:S(2)}, u32[]{:S(2)}) %all-to-all-start) | async-done | bytes 16777248 | tf_op jit(solution)/shard_map/all_to_all | solution.py:108
  628.0 33.4 %convolution_bitcast_fusion = f32[16,1,256,1536]{3,2,0,1:T(8,128)} fusion(bf16[16,256,2048]{2,1,0:T(8,128)(2,1)} %all-to-all-done, bf16[1,2048,1536]{2,1,0:T(8,128)(2,1)} %param.28), kind=kOutput, calls=%fused_computation.21 | convolution fusion | flops 25769803776 | bytes 48234496 | tf_op jit(solution)/shard_map/sjcd,jdf->sjcf/dot_general | solution.py:261
  661.4 357.8 %all-to-all-done.2 = bf16[16,256,2048]{2,1,0:T(8,128)(2,1)} async-done(((bf16[16,256,2048]{2,1,0:T(8,128)(2,1)}), bf16[16,256,2048]{2,1,0:T(8,128)(2,1)}, u32[]{:S(2)}, u32[]{:S(2)}) %all-to-all-start.2) | async-done | bytes 16777248 | tf_op jit(solution)/shard_map/all_to_all | solution.py:108
  1019.2 30.3 %fusion.34 = (bf16[16,256,768]{2,1,0:T(8,128)(2,1)}, bf16[16,256,768]{2,1,0:T(8,128)(2,1)}, bf16[16,1,256,768]{3,2,0,1:T(8,128)(2,1)}) fusion(f32[16,1,256,1536]{3,2,0,1:T(8,128)} %convolution_bitcast_fusion, bf16[16,256,2048]{2,1,0:T(8,128)(2,1)} %all-to-all-done.2, bf16[1,768,2048]{2,1,0:T(8,128)(2,1)S(1)} %copy-done), kind=kOutput, calls=%fused_computation.68 | convolution fusion | flops 12935233536 | bytes 63963136 | tf_op jit(solution)/shard_map/sjcd,jfd->sjcf/dot_general | solution.py:296
  1073.7 32.5 %convolution_convert_fusion.1 = bf16[16,256,2048]{2,1,0:T(8,128)(2,1)} fusion(bf16[16,256,768]{2,1,0:T(8,128)(2,1)} %get-tuple-element.47, bf16[16,256,768]{2,1,0:T(8,128)(2,1)} %get-tuple-element.46, bf16[1,2048,1536]{2,1,0:T(8,128)(2,1)} %param.28), kind=kOutput, calls=%fused_computation.28 | convolution fusion | flops 25803358208 | bytes 35651584 | tf_op jit(solution)/shard_map/sjcf,jdf->sjcd/dot_general | solution.py:309
  1106.2 358.7 %all-to-all-done.1 = bf16[16,256,2048]{2,1,0:T(8,128)(2,1)} async-done(((bf16[16,256,2048]{2,1,0:T(8,128)(2,1)}), bf16[16,256,2048]{2,1,0:T(8,128)(2,1)}, u32[]{:S(2)}, u32[]{:S(2)}) %all-to-all-start.1) | async-done | bytes 16777248 | tf_op jit(solution)/shard_map/all_to_all | solution.py:108
  1470.2 50.2 %gather_fusion = bf16[2048,2048]{1,0:T(8,128)(2,1)} fusion(bf16[16,256,2048]{2,1,0:T(8,128)(2,1)} %all-to-all-done.1, s32[2048]{0:T(1024)S(1)} %bitcast.348), kind=kCustom, calls=%fused_computation | custom fusion | bytes 16793600 | tf_op jit(solution)/shard_map/gather | solution.py:272
  1530.3 331.1 %all-to-all-done.3 = bf16[16,256,2048]{2,1,0:T(8,128)(2,1)} async-done(((bf16[16,256,2048]{2,1,0:T(8,128)(2,1)}), bf16[16,256,2048]{2,1,0:T(8,128)(2,1)}, u32[]{:S(2)}, u32[]{:S(2)}) %all-to-all-start.3) | async-done | bytes 16777248 | tf_op jit(solution)/shard_map/all_to_all | solution.py:108
  1861.4 50.4 %gather_fusion.1 = bf16[2048,2048]{1,0:T(8,128)(2,1)} fusion(bf16[16,256,2048]{2,1,0:T(8,128)(2,1)} %all-to-all-done.3, s32[2048]{0:T(1024)S(1)} %bitcast.349), kind=kCustom, calls=%fused_computation.1 | custom fusion | bytes 16793600 | tf_op jit(solution)/shard_map/gather | solution.py:314
  1933.0 47.1 %all-gather.5.cloned.1.call-done = bf16[1024,2048]{1,0:T(8,128)(2,1)} async-done(((bf16[256,2048]{1,0:T(8,128)(2,1)}), bf16[1024,2048]{1,0:T(8,128)(2,1)}) %all-gather.5.cloned.1.call-update) | async-done | bytes 4194320 | tf_op jit(solution)/shard_map/all_gather | solution.py:333
  1991.8 49.3 %fusion = (f32[8,1024]{1,0:T(8,128)S(1)}, f32[2048,1024,8]{1,0,2:T(8,128)}) fusion(f32[8,1024]{1,0:T(8,128)S(1)} %copy-done.57, f32[2048,1024,8]{1,0,2:T(8,128)} %get-tuple-element.92, pred[1024,2048]{0,1:T(8,128)(4,1)S(1)} %copy-done.17, bf16[256,1,8,128]{3,0,2,1:T(8,128)(2,1)} %copy.142, bf16[256,1,8,128]{3,0,2,1:T(8,128)(2,1)} %copy.141, ...), kind=kOutput, calls=%fused_computation.7 | convolution fusion | flops 4401913856 | bytes 139001856 | tf_op jit(solution)/shard_map/qkgd,tkd->kgqt/dot_general | solution.py:364
  2041.1 28.3 %fusion.55 = bf16[2048,128]{0,1:T(8,128)(2,1)} fusion(bf16[256,1,8,128]{3,0,2,1:T(8,128)(2,1)} %copy.142, bf16[256,1,8,128]{3,0,2,1:T(8,128)(2,1)} %copy.141, bf16[512,1,8,128]{3,0,2,1:T(8,128)(2,1)S(1)} %copy-done.48, f32[8,1024]{1,0:T(8,128)S(1)} %copy-done.57, f32[2048,1024,8]{1,0,2:T(8,128)} %get-tuple-element.92, pred[1024,2048]{0,1:T(8,128)(4,1)S(1)} %copy-done.17), kind=kOutput, calls=%fused_computation.102 | convolution fusion | flops 4385406976 | bytes 71860224 | tf_op jit(solution)/shard_map/kgqt,qkgd->tkd/dot_general | solution.py:358
  2069.4 53.4 %fusion.4 = bf16[8,1024,2048]{1,2,0:T(8,128)(2,1)} fusion(f32[2048,1024,8]{1,0,2:T(8,128)} %get-tuple-element.95, f32[8,1024]{1,0:T(8,128)S(1)} %get-tuple-element.94, f32[8,1024]{1,0:T(8,128)S(1)} %copy-done.57, f32[2048,1024,8]{1,0,2:T(8,128)} %get-tuple-element.92, pred[1024,2048]{0,1:T(8,128)(4,1)S(1)} %copy-done.17), kind=kLoop, calls=%fused_computation.13 | loop fusion | flops 117440512 | bytes 169934848 | tf_op jit(solution)/shard_map/reshape.32
  2200.4 45.6 %all-reduce.15.cloned.1.call-done = (bf16[1024,512]{0,1:T(8,128)(2,1)}, bf16[1024,512]{0,1:T(8,128)(2,1)}) async-done(((bf16[1024,512]{0,1:T(8,128)(2,1)}, bf16[1024,512]{0,1:T(8,128)(2,1)}), (bf16[1024,512]{0,1:T(8,128)(2,1)}, bf16[1024,512]{0,1:T(8,128)(2,1)})) %all-reduce.15.cloned.1.call-update) | async-done | bytes 2097168 | tf_op jit(solution)/shard_map/psum | solution.py:406
  2289.6 34.2 %fusion.27 = bf16[1,2048,1536]{2,1,0:T(8,128)(2,1)} fusion(bf16[16,256,2048]{2,1,0:T(8,128)(2,1)} %all-to-all-done, bf16[16,256,768]{2,1,0:T(8,128)(2,1)} %get-tuple-element.47, bf16[16,256,768]{2,1,0:T(8,128)(2,1)} %get-tuple-element.46), kind=kOutput, calls=%fused_computation.58 | convolution fusion | flops 25798115328 | bytes 35651584 | tf_op jit(solution)/shard_map/sjcd,sjcf->jdf/dot_general | solution.py:306
  2348.5 26.2 all-reduce.13.cloned.1.call-done
  2374.7 43.9 %all-reduce.17.cloned.1.call-done = (bf16[1,2048,1536]{2,1,0:T(8,128)(2,1)}, bf16[1,768,2048]{2,1,0:T(8,128)(2,1)}) async-done(((bf16[1,2048,1536]{2,1,0:T(8,128)(2,1)}, bf16[1,768,2048]{2,1,0:T(8,128)(2,1)}), (bf16[1,2048,1536]{2,1,0:T(8,128)(2,1)}, bf16[1,768,2048]{2,1,0:T(8,128)(2,1)})) %all-reduce.17.cloned.1.call-update) | async-done | bytes 9437200 | tf_op jit(solution)/shard_map/psum | solution.py:460
  2434.9 40.1 %all-gather.3.cloned.1.call-done = bf16[1024,2048]{1,0:T(8,128)(2,1)} async-done(((bf16[256,2048]{1,0:T(8,128)(2,1)}), bf16[1024,2048]{1,0:T(8,128)(2,1)}) %all-gather.3.cloned.1.call-update) | async-done | bytes 4194320 | tf_op jit(solution)/shard_map/all_gather | solution.py:330
  2519.7 217.7 %all-reduce.11.cloned.1.call-done = (bf16[2048,1024]{1,0:T(8,128)(2,1)}, bf16[2048,512]{1,0:T(8,128)(2,1)}, bf16[2048,512]{1,0:T(8,128)(2,1)}, bf16[1024,2048]{1,0:T(8,128)(2,1)}, bf16[2048,16]{0,1:T(8,128)(2,1)}) async-done(((bf16[2048,1024]{1,0:T(8,128)(2,1)}, bf16[2048,512]{1,0:T(8,128)(2,1)}, bf16[2048,512]{1,0:T(8,128)(2,1)}, bf16[1024,2048]{1,0:T(8,128)(2,1)}, bf16[2048,16]{0,1:T(8,128)(2,1)}), ...) | async-done | bytes 12648464 | tf_op jit(solution)/shard_map/psum | solution.py:449
  (360 shorter events, 431.4 us)
Async XLA Ops:
  7.2 1012.1 %copy-start = (bf16[1,768,2048]{2,1,0:T(8,128)(2,1)S(1)}, bf16[1,768,2048]{2,1,0:T(8,128)(2,1)}, u32[]{:S(2)}) copy-start(bf16[1,768,2048]{2,1,0:T(8,128)(2,1)} %param.29) | copy-start | bytes 9437188
  7.2 193.6 %reduce-scatter.4.cloned.1.call-start = ((), (), s32[]{:S(2)}) async-start(), calls=%async_computation.7 | async-start | bytes 5242880 | tf_op jit(solution)/shard_map/reduce_scatter | solution.py:222
  40.9 26.6 copy-start.29
  40.9 26.6 copy-start.30
  89.9 32.5 %copy-start.56 = (f32[8,1024]{1,0:T(8,128)}, f32[8,1024]{1,0:T(8,128)S(1)}, u32[]{:S(2)}) copy-start(f32[8,1024]{1,0:T(8,128)S(1)} %log_add_fusion) | copy-start | bytes 98308
  96.0 26.5 copy-start.51
  146.3 97.5 %copy-start.58 = (s32[256,8]{0,1:T(8,128)}, s32[256,8]{0,1:T(8,128)S(1)}, u32[]{:S(2)}) copy-start(s32[256,8]{0,1:T(8,128)S(1)} %constant_dynamic-slice_fusion.1) | copy-start | bytes 24580
  166.6 37.8 %copy-start.62 = (f32[2048]{0:T(1024)S(1)}, f32[2048]{0:T(1024)}, u32[]{:S(2)}) copy-start(f32[2048]{0:T(1024)} %param.26) | copy-start | bytes 24580
  227.9 395.0 %all-to-all-start = ((bf16[16,256,2048]{2,1,0:T(8,128)(2,1)}), bf16[16,256,2048]{2,1,0:T(8,128)(2,1)}, u32[]{:S(2)}, u32[]{:S(2)}) async-start(bf16[16,256,2048]{2,1,0:T(8,128)(2,1)} %bitcast.350), calls=%async_computation.1 | async-start | bytes 33554432 | tf_op jit(solution)/shard_map/all_to_all | solution.py:108
  622.9 396.3 %all-to-all-start.2 = ((bf16[16,256,2048]{2,1,0:T(8,128)(2,1)}), bf16[16,256,2048]{2,1,0:T(8,128)(2,1)}, u32[]{:S(2)}, u32[]{:S(2)}) async-start(bf16[16,256,2048]{2,1,0:T(8,128)(2,1)} %bitcast.351), calls=%async_computation.3 | async-start | bytes 33554432 | tf_op jit(solution)/shard_map/all_to_all | solution.py:108
  1068.6 396.4 %all-to-all-start.1 = ((bf16[16,256,2048]{2,1,0:T(8,128)(2,1)}), bf16[16,256,2048]{2,1,0:T(8,128)(2,1)}, u32[]{:S(2)}, u32[]{:S(2)}) async-start(bf16[16,256,2048]{2,1,0:T(8,128)(2,1)} %convolution_convert_fusion), calls=%async_computation.2 | async-start | bytes 33554432 | tf_op jit(solution)/shard_map/all_to_all | solution.py:108
  1106.2 363.9 %copy-start.2 = (s32[2048,1]{0,1:T(1,128)S(1)}, s32[2048,1]{0,1:T(1,128)}, u32[]{:S(2)}) copy-start(s32[2048,1]{0,1:T(1,128)} %get-tuple-element.81) | copy-start | bytes 24580
  1464.9 396.4 %all-to-all-start.3 = ((bf16[16,256,2048]{2,1,0:T(8,128)(2,1)}), bf16[16,256,2048]{2,1,0:T(8,128)(2,1)}, u32[]{:S(2)}, u32[]{:S(2)}) async-start(bf16[16,256,2048]{2,1,0:T(8,128)(2,1)} %convolution_convert_fusion.1), calls=%async_computation.4 | async-start | bytes 33554432 | tf_op jit(solution)/shard_map/all_to_all | solution.py:108
  1470.1 510.1 %all-gather.5.cloned.1.call-start = ((), (), s32[]{:S(2)}) async-start(), calls=%async_computation.9 | async-start | bytes 5242880 | tf_op jit(solution)/shard_map/all_gather | solution.py:333
  1470.2 50.2 %copy-start.18 = (f32[256,2048]{1,0:T(8,128)S(1)}, f32[256,2048]{1,0:T(8,128)}, u32[]{:S(2)}) copy-start(f32[256,2048]{1,0:T(8,128)} %constant_dynamic-slice_fusion) | copy-start | bytes 6291460
  1470.2 50.2 %copy-start.47 = (f32[256,8]{1,0:T(8,128)S(1)}, f32[256,8]{1,0:T(8,128)}, u32[]{:S(2)}) copy-start(f32[256,8]{1,0:T(8,128)} %copy-done.46) | copy-start | bytes 24580
  1931.0 232.1 %reduce-scatter.6.cloned.1.call-start = ((), (), s32[]{:S(2)}) async-start(), calls=%async_computation.10 | async-start | bytes 786432 | tf_op jit(solution)/shard_map/reduce_scatter | solution.py:378
  1991.8 49.3 %copy-start.48 = (bf16[512,1,8,128]{3,0,2,1:T(8,128)(2,1)S(1)}, bf16[512,1,8,128]{3,0,2,1:T(8,128)(2,1)}, u32[]{:S(2)}) copy-start(bf16[512,1,8,128]{3,0,2,1:T(8,128)(2,1)} %copy.140) | copy-start | bytes 3145732
  2143.1 28.0 %reduce-scatter.8.cloned.1.call-start = ((), (), s32[]{:S(2)}) async-start(), calls=%async_computation.11 | async-start | bytes 786432 | tf_op jit(solution)/shard_map/reduce_scatter | solution.py:384
  2163.0 82.9 %all-reduce.15.cloned.1.call-start = ((), (), s32[]{:S(2)}) async-start(), calls=%async_computation.14 | async-start | bytes 4194304 | tf_op jit(solution)/shard_map/psum | solution.py:406
  2173.2 201.5 %all-reduce.13.cloned.1.call-start = ((), (), s32[]{:S(2)}) async-start(), calls=%async_computation.13 | async-start | bytes 8519680 | tf_op jit(solution)/shard_map/psum | solution.py:438
  2269.2 149.4 %all-reduce.17.cloned.1.call-start = ((), (), s32[]{:S(2)}) async-start(), calls=%async_computation.15 | async-start | bytes 18874368 | tf_op jit(solution)/shard_map/psum | solution.py:460
  2323.8 151.1 %all-gather.3.cloned.1.call-start = ((), (), s32[]{:S(2)}) async-start(), calls=%async_computation.8 | async-start | bytes 5242880 | tf_op jit(solution)/shard_map/all_gather | solution.py:330
  2324.6 412.9 %all-reduce.11.cloned.1.call-start = ((), (), s32[]{:S(2)}) async-start(), calls=%async_computation.12 | async-start | bytes 25296896 | tf_op jit(solution)/shard_map/psum | solution.py:449
  (85 other events, 592.7 us)
Sparse Core Ops, SparseCore 0:
  145.4 55.3 reduce-scatter.3
  1931.1 49.0 all-gather.4
  2143.1 7.9 reduce-scatter.5
  2163.1 7.9 reduce-scatter.7
  2174.9 70.9 all-reduce.14
  2269.3 105.2 all-reduce.12
  2377.8 40.7 all-reduce.16
  2421.1 53.8 all-gather.2
  2478.3 259.1 all-reduce.10
where the time goes:
time: 2770 us; the launch traced here: 2760 us
  waiting for transfers between devices  1860 us (67%)
  matrix products  414 us (15%)
  other arithmetic  228 us (8%)
  local copies, waits for them, and re-layouts  187 us (7%)
  blocking collectives  32.2 us (1%)
    all_to_all x4, waiting for transfers between devices, move_slots(): lax.all_to_all(slot_rows, ('expert', 'dp'), split_axis=0, concat_axis=0,...  1400 us
    psum x1, waiting for transfers between devices, on_device(): lax.psum(query_weight_grad.astype(jnp.bfloat16), ('ctx', 'dp'))  218 us
    another operation x5, other arithmetic  59.7 us
  transfers between devices with their start and end apart: 13, of which 12 were waited for; matrix products, arithmetic and copies ran while one was open for 12% of the time, Pallas kernels for 0%

commit v1 on v0

v1 whole, which is shorter than its diff:
```python
import functools
import math

import jax
import jax.numpy as jnp
from jax import lax
from jax.experimental import pallas as pl
from jax.experimental.pallas import tpu as pltpu
from jax.sharding import PartitionSpec as P

H = 32
KV = 4
P_SIZE = 1024


NORM_EPS = 1e-06
ROPE_BASE = 1000000.0
HIGHEST = lax.Precision.HIGHEST
LOG2E = math.log2(math.e)


def rms_scaled(values, gain_row):
    return (
        values * lax.rsqrt(jnp.mean(values * values, axis=-1, keepdims=True) + NORM_EPS) * gain_row
    )


def rms_backward(values, gain_row, upstream):
    inverse = lax.rsqrt(jnp.mean(values * values, axis=-1, keepdims=True) + NORM_EPS)
    unit_rows = values * inverse
    scaled = upstream * gain_row
    inner_mean = jnp.mean(scaled * unit_rows, axis=-1, keepdims=True)
    return (inverse * (scaled - unit_rows * inner_mean), upstream * unit_rows)


def rotary_tables(positions, head_width):
    halfway = head_width // 2
    frequency = jnp.exp(
        jnp.arange(halfway, dtype=jnp.float32) * (-2.0 * math.log(ROPE_BASE) / head_width)
    )
    angles = positions[:, None] * frequency[None, :]
    cosine, sine = jnp.cos(angles), jnp.sin(angles)
    return (jnp.concatenate([cosine, cosine], 1), jnp.concatenate([-sine, sine], 1))


def f32(values):
    return values.astype(jnp.float32)


def low(values):
    return values.astype(jnp.bfloat16)


def ring_gather(own, axis, size):
    held = [own]
    for _ in range(size - 1):
        held.append(lax.ppermute(held[-1], axis, [(j, (j + 1) % size) for j in range(size)]))
    return held


def ring_scatter(parts, axis, size):
    if size == 1:
        return f32(parts[0])
    total = parts[1]
    for s in range(2, size + 1):
        total = lax.ppermute(total, axis, [(j, (j + 1) % size) for j in range(size)])
        total = f32(total) + f32(parts[s % size])
        if s < size:
            total = total.astype(parts[0].dtype)
    return total


def cube_bits(size):
    return [1 << k for k in range(size.bit_length() - 1)]


def cube_gather(own, axis, size, bits):
    held = {0: own}
    for bit in bits:
        for r in list(held):
            held[r ^ bit] = lax.ppermute(held[r], axis, [(j, j ^ bit) for j in range(size)])
    return [held[r] for r in range(size)]


def cube_gather_halves(own, axis, size):
    half = own.shape[0] // 2
    bits = cube_bits(size)
    first = cube_gather(own[:half], axis, size, bits)
    second = cube_gather(own[half:], axis, size, bits[::-1])
    return list(zip(first, second))


def cube_scatter(parts, axis, size, bits):
    held = dict(enumerate(parts))
    for bit in bits:
        for r in [r for r in held if r & bit]:
            there = lax.ppermute(low(held.pop(r)), axis, [(j, j ^ bit) for j in range(size)])
            total = f32(held[r ^ bit]) + f32(there)
            held[r ^ bit] = total if bit == bits[-1] else low(total)
    return f32(held[0])


def cube_scatter_halves(parts, axis, size):
    half = parts[0].shape[0] // 2
    bits = cube_bits(size)
    first = cube_scatter([p[:half] for p in parts], axis, size, bits)
    second = cube_scatter([p[half:] for p in parts], axis, size, bits[::-1])
    return jnp.concatenate([first, second], axis=0)


def swap(values, axis):
    return lax.ppermute(values, axis, [(0, 1), (1, 0)])


def to_cube(rows, index, size):
    share = rows.shape[0] // size
    return jnp.concatenate(
        [lax.dynamic_slice_in_dim(rows, (index ^ r) * share, share, 0) for r in range(size)], axis=0
    )


def from_cube(blocks, index):
    share = sum(b.shape[0] for b in blocks[0])
    whole = jnp.zeros((len(blocks) * share,) + blocks[0][0].shape[1:], blocks[0][0].dtype)
    for r, pieces in enumerate(blocks):
        at = (index ^ r) * share
        for piece in pieces:
            whole = lax.dynamic_update_slice_in_dim(whole, piece, at, 0)
            at = at + piece.shape[0]
    return whole


def dot_nn(a,b): return lax.dot_general(a,b,(((1,),(0,)),((),())),preferred_element_type=jnp.float32)
def dot_nt(a,b): return lax.dot_general(a,b,(((1,),(1,)),((),())),preferred_element_type=jnp.float32)

def moe_kernel(n_units, halves, pieces, *refs):
    n_w = sum(len(p) for p in pieces)
    x_ref, u_ref, gates_ref, router_ref = refs[:4]
    w_refs = refs[4:4 + n_w]
    (mix_ref, row_ref, coef_ref, act_ref, dgu_ref, gu_buf, d_buf, mix_acc, row_acc, gg_acc, sems) = refs[-11:]
    unit = pl.program_id(0)
    width = d_buf.shape[1] // halves

    def copies(k, slot):
        base = sum(len(p) for p in pieces[:k])
        out = []
        for j, (kind, half, off, size) in enumerate(pieces[k]):
            if kind == 0:
                dst = gu_buf.at[slot, pl.ds(off, size), pl.ds(half * 2 * width, 2 * width)]
            else:
                dst = d_buf.at[slot, pl.ds(half * width + off, size)]
            out.append(pltpu.make_async_copy(w_refs[base + j], dst, sems.at[slot, j]))
        return out

    @pl.when(unit == 0)
    def _():
        for c in copies(0, 0):
            c.start()
        mix_acc[...] = jnp.zeros_like(mix_acc)
        row_acc[...] = jnp.zeros_like(row_acc)
        gg_acc[...] = jnp.zeros_like(gg_acc)

    for k in range(n_units):
        @pl.when(unit == k)
        def _(k=k):
            if k + 1 < n_units:
                for c in copies(k + 1, (k + 1) % 2):
                    c.start()
            for c in copies(k, k % 2):
                c.wait()

    slot = lax.rem(unit, 2)
    gates = gates_ref[...]
    lane = lax.broadcasted_iota(jnp.int32, gates.shape, 1)
    here = lane == unit
    gate = jnp.sum(jnp.where(here, gates, 0.0), axis=1, keepdims=True)
    x = x_ref[...]
    u = u_ref[...]
    acts, dgus = [], []
    gg = 0.0
    for h in range(halves):
        gu = gu_buf[slot, :, h * 2 * width:(h + 1) * 2 * width]
        d = d_buf[slot, h * width:(h + 1) * width]
        pre = dot_nn(x, gu)
        back = dot_nt(u, d)
        g_part = pre[:, :width]
        u_part = pre[:, width:]
        sig = 1.0 / (1.0 + jnp.exp(-g_part))
        silu = g_part * sig
        active = silu * u_part
        acts.append((active * gate).astype(jnp.bfloat16))
        gg = gg + jnp.sum(active * back, axis=1, keepdims=True)
        ag = back * gate
        dgus.append((ag * u_part * (sig + silu * (1.0 - sig))).astype(jnp.bfloat16))
        dgus.append((ag * silu).astype(jnp.bfloat16))
    act = jnp.concatenate(acts, axis=1)
    dgu = jnp.concatenate(dgus, axis=1)
    gg_acc[...] += jnp.where(here, gg, 0.0)
    act_ref[0] = act
    dgu_ref[0] = dgu
    mix_acc[...] += dot_nn(act, d_buf[slot])
    row_acc[...] += dot_nt(dgu, gu_buf[slot])

    @pl.when(unit == n_units - 1)
    def _():
        coef = gates * gg_acc[...]
        coef_ref[...] = coef
        mix_ref[...] = mix_acc[...].astype(jnp.bfloat16)
        extra = dot_nn(coef.astype(jnp.bfloat16), router_ref[...])
        row_ref[...] = (row_acc[...] + extra).astype(jnp.bfloat16)

def moe_rows(x, u, gates, router_rows, units, halves, slot_at, slots, kept):
    rows, width = x.shape
    n_units = len(units)
    pieces = [[(k, h, o, a.shape[0]) for k, h, o, a in unit] for unit in units]
    arrays = [a for unit in units for _, _, _, a in unit]
    hidden = sum(a.shape[0] for k, h, o, a in units[0] if k == 1)
    most = max(len(p) for p in pieces)
    any_spec = pl.BlockSpec(memory_space=pl.ANY)
    whole = lambda shape: pl.BlockSpec(shape, lambda i: (0,) * len(shape))
    in_specs = [whole(x.shape), whole(u.shape), whole(gates.shape), whole(router_rows.shape)] + [any_spec] * len(arrays)
    operands = [x, u, gates, router_rows] + arrays
    aliases = {}
    if kept is not None:
        in_specs += [any_spec, any_spec]
        aliases = {len(operands): 3, len(operands) + 1: 4}
        operands += list(kept)
    f32 = jnp.float32
    flops = 2 * rows * width * hidden * 6 * n_units
    return pl.pallas_call(
        functools.partial(moe_kernel, n_units, halves, pieces),
        grid=(n_units,),
        in_specs=in_specs,
        out_specs=[whole((rows, width)), whole((rows, width)), whole((rows, 128)),
            pl.BlockSpec((1, rows, hidden), lambda i: (i, slot_at, 0)),
            pl.BlockSpec((1, rows, 2 * hidden), lambda i: (i, slot_at, 0))],
        out_shape=[jax.ShapeDtypeStruct((rows, width), jnp.bfloat16), jax.ShapeDtypeStruct((rows, width), jnp.bfloat16),
            jax.ShapeDtypeStruct((rows, 128), f32),
            jax.ShapeDtypeStruct((n_units, slots * rows, hidden), jnp.bfloat16),
            jax.ShapeDtypeStruct((n_units, slots * rows, 2 * hidden), jnp.bfloat16)],
        scratch_shapes=[pltpu.VMEM((2, width, 2 * hidden), jnp.bfloat16), pltpu.VMEM((2, hidden, width), jnp.bfloat16),
            pltpu.VMEM((rows, width), f32), pltpu.VMEM((rows, width), f32), pltpu.VMEM((rows, 128), f32),
            pltpu.SemaphoreType.DMA((2, most))],
        input_output_aliases=aliases,
        compiler_params=pltpu.CompilerParams(vmem_limit_bytes=56 * 1024 * 1024, dimension_semantics=("arbitrary",)),
        cost_estimate=pl.CostEstimate(flops=flops, bytes_accessed=sum(a.size * 2 for a in arrays), transcendentals=0),
    )(*operands)


def key_row(t, block, prompt_blocks, segment, segment_rows):
    later = prompt_blocks * block + segment * segment_rows + (t - prompt_blocks) * block
    return pl.multiple_of(jnp.where(t < prompt_blocks, t * block, later), block)

def block_plan(own, block, prompt_blocks, own_prompt):
    at = pl.program_id(0)
    is_prompt = at < own_prompt
    full = jnp.where(is_prompt, own * own_prompt + at, prompt_blocks + own)
    return full, jnp.maximum(at - own_prompt, 0)

def turn(values, cosine, sine):
    half = values.shape[-1] // 2
    return values * cosine + jnp.concatenate([values[:, half:], values[:, :half]], axis=-1) * sine

def fwd_kernel(heads, block, prompt_blocks, own_prompt, segment_rows, scale,
               own_ref, pre_ref, gain_ref, cos_ref, sin_ref, k_ref, v_ref, q_ref, out_ref, lse_ref, acc):
    full, segment = block_plan(own_ref[0], block, prompt_blocks, own_prompt)
    width = k_ref.shape[1]
    cosine, sine, gain = cos_ref[...], sin_ref[...], gain_ref[...]
    for h in range(heads):
        pre = pre_ref[:, h * width:(h + 1) * width]
        unit = pre * lax.rsqrt(jnp.mean(pre * pre, axis=1, keepdims=True) + NORM_EPS) * gain
        q_ref[h] = (turn(unit, cosine, sine) * scale).astype(jnp.bfloat16)
    acc[...] = jnp.zeros_like(acc)

    def step(t, masked):
        first = key_row(t, block, prompt_blocks, segment, segment_rows)
        keys = k_ref[pl.ds(first, block)]
        values = jnp.concatenate([v_ref[pl.ds(first, block)], jnp.ones((block, width), jnp.bfloat16)], axis=1)
        for h in range(heads):
            p = jnp.exp2(dot_nt(q_ref[h], keys))
            if masked:
                p = jnp.where(lax.broadcasted_iota(jnp.int32, p.shape, 1) <= lax.broadcasted_iota(jnp.int32, p.shape, 0), p, 0.0)
            acc[h] += dot_nn(p.astype(jnp.bfloat16), values)

    @pl.loop(0, full)
    def _(t):
        step(t, False)
    step(full, True)
    for h in range(heads):
        total = acc[h, :, width:]
        out_ref[:, h * width:(h + 1) * width] = (acc[h, :, :width] / total).astype(jnp.bfloat16)
        lse_ref[h:h + 1] = jnp.log2(total).T[:1]

def bwd_kernel(heads, block, prompt_blocks, own_prompt, segment_rows, scale,
               own_ref, q_ref, k_ref, kt_ref, v_ref, lse_ref, out_ref, do_ref, pre_ref, gain_ref, cos_ref, sin_ref,
               dpre_ref, dk_ref, dv_ref, dgain_ref, acc, delta):
    full, segment = block_plan(own_ref[0], block, prompt_blocks, own_prompt)
    width = k_ref.shape[1]

    @pl.when(pl.program_id(0) == 0)
    def _():
        dk_ref[...] = jnp.zeros_like(dk_ref)
        dv_ref[...] = jnp.zeros_like(dv_ref)
        dgain_ref[...] = jnp.zeros_like(dgain_ref)

    for h in range(heads):
        cols = slice(h * width, (h + 1) * width)
        prod = out_ref[:, cols].astype(jnp.float32) * do_ref[:, cols].astype(jnp.float32)
        delta[h:h + 1] = jnp.sum(prod.T, axis=0, keepdims=True)
    acc[...] = jnp.zeros_like(acc)

    def step(t, masked):
        first = key_row(t, block, prompt_blocks, segment, segment_rows)
        rows = pl.ds(first, block)
        keys = k_ref[rows]
        kt = kt_ref[:, rows]
        values = v_ref[rows]
        dk = dv = 0.0
        for h in range(heads):
            q = q_ref[h]
            do = do_ref[:, h * width:(h + 1) * width]
            p = jnp.exp2(dot_nt(keys, q) - lse_ref[h:h + 1])
            if masked:
                p = jnp.where(lax.broadcasted_iota(jnp.int32, p.shape, 0) <= lax.broadcasted_iota(jnp.int32, p.shape, 1), p, 0.0)
            ds = (p * (dot_nt(values, do) - delta[h:h + 1])).astype(jnp.bfloat16)
            dv += dot_nn(p.astype(jnp.bfloat16), do)
            dk += dot_nn(ds, q)
            acc[h] += dot_nn(kt, ds)
        dk_ref[rows] += dk
        dv_ref[rows] += dv

    @pl.loop(0, full)
    def _(t):
        step(t, False)
    step(full, True)
    cosine, sine, gain = cos_ref[...], sin_ref[...], gain_ref[...]
    dgain = 0.0
    for h in range(heads):
        cols = slice(h * width, (h + 1) * width)
        turned = turn(acc[h].T * scale, cosine, -sine)
        pre = pre_ref[:, cols]
        inverse = lax.rsqrt(jnp.mean(pre * pre, axis=1, keepdims=True) + NORM_EPS)
        unit = pre * inverse
        scaled = turned * gain
        dpre_ref[:, cols] = (inverse * (scaled - unit * jnp.mean(scaled * unit, axis=1, keepdims=True))).astype(jnp.bfloat16)
        dgain = dgain + jnp.sum(turned * unit, axis=0, keepdims=True)
    dgain_ref[...] += dgain

def attend(own, pre, gain, cosine, sine, keys, values, block, prompt_total, heads):
    rows = pre.shape[0]
    head = keys.shape[1]
    width = heads * head
    own_prompt = rows // block - 2
    segment_rows = (keys.shape[0] - prompt_total) // 2
    scale = LOG2E / math.sqrt(head)
    whole = lambda shape: pl.BlockSpec(shape, lambda i, s: (0,) * len(shape))
    row = lambda w: pl.BlockSpec((block, w), lambda i, s: (i, 0))
    return pl.pallas_call(
        functools.partial(fwd_kernel, heads, block, prompt_total // block, own_prompt, segment_rows, scale),
        grid_spec=pltpu.PrefetchScalarGridSpec(
            num_scalar_prefetch=1, grid=(rows // block,),
            in_specs=[row(width), whole((1, head)), row(head), row(head), whole(keys.shape), whole(values.shape)],
            out_specs=[pl.BlockSpec((heads, block, head), lambda i, s: (0, i, 0)), row(width),
                       pl.BlockSpec((heads, block), lambda i, s: (0, i))],
            scratch_shapes=[pltpu.VMEM((heads, block, 2 * head), jnp.float32)]),
        out_shape=[jax.ShapeDtypeStruct((heads, rows, head), jnp.bfloat16), jax.ShapeDtypeStruct((rows, width), jnp.bfloat16),
                   jax.ShapeDtypeStruct((heads, rows), jnp.float32)],
        compiler_params=pltpu.CompilerParams(vmem_limit_bytes=40 * 1024 * 1024, dimension_semantics=("arbitrary",)),
        cost_estimate=pl.CostEstimate(flops=2 * rows * keys.shape[0] * width * 2, bytes_accessed=rows * width * 10, transcendentals=rows * keys.shape[0] * heads // 2),
    )(own, pre, gain, cosine, sine, keys, values)

def attend_back(own, q, keys, keys_t, values, lse, out, dout, pre, gain, cosine, sine, block, prompt_total):
    rows, width = out.shape
    head = keys.shape[1]
    heads = width // head
    own_prompt = rows // block - 2
    segment_rows = (keys.shape[0] - prompt_total) // 2
    whole = lambda shape: pl.BlockSpec(shape, lambda i, s: (0,) * len(shape))
    row = lambda w: pl.BlockSpec((block, w), lambda i, s: (i, 0))
    return pl.pallas_call(
        functools.partial(bwd_kernel, heads, block, prompt_total // block, own_prompt, segment_rows, 1.0 / math.sqrt(head)),
        grid_spec=pltpu.PrefetchScalarGridSpec(
            num_scalar_prefetch=1, grid=(rows // block,),
            in_specs=[pl.BlockSpec((heads, block, head), lambda i, s: (0, i, 0)), whole(keys.shape), whole(keys_t.shape), whole(values.shape),
                      pl.BlockSpec((heads, block), lambda i, s: (0, i)), row(width), row(width), row(width), whole((1, head)), row(head), row(head)],
            out_specs=[row(width), whole(keys.shape), whole(keys.shape), whole((1, head))],
            scratch_shapes=[pltpu.VMEM((heads, head, block), jnp.float32), pltpu.VMEM((heads, block), jnp.float32)]),
        out_shape=[jax.ShapeDtypeStruct((rows, width), jnp.bfloat16), jax.ShapeDtypeStruct(keys.shape, jnp.float32),
                   jax.ShapeDtypeStruct(keys.shape, jnp.float32), jax.ShapeDtypeStruct((1, head), jnp.float32)],
        compiler_params=pltpu.CompilerParams(vmem_limit_bytes=40 * 1024 * 1024, dimension_semantics=("arbitrary",)),
        cost_estimate=pl.CostEstimate(flops=2 * rows * keys.shape[0] * width * 5, bytes_accessed=rows * width * 12, transcendentals=rows * keys.shape[0] * heads // 2),
    )(own, q, keys, keys_t, values, lse, out, dout, pre, gain, cosine, sine)


def weight_units(gate_up, down, expert_parts, ctx_parts, ctx_index):
    hidden = down.shape[0]
    halves = 2 if ctx_parts == 2 else 1
    width = hidden // halves

    def half_of(which):
        gate = lax.dynamic_slice_in_dim(gate_up, which * width, width, 1)
        up = lax.dynamic_slice_in_dim(gate_up, hidden + which * width, width, 1)
        return (
            jnp.concatenate([gate, up], axis=1),
            lax.dynamic_slice_in_dim(down, which * width, width, 0),
        )

    if halves == 2:
        mine, other = half_of(ctx_index), half_of(1 - ctx_index)
    else:
        mine, other = (gate_up, down), None
    units = []
    downs = cube_gather_halves(mine[1], "expert", expert_parts)
    ups = cube_gather_halves(mine[0], "expert", expert_parts)
    for r in range(expert_parts):
        unit = []
        if r == 0:
            sides = [([mine[0]], [mine[1]])] + ([([other[0]], [other[1]])] if halves == 2 else [])
        else:
            sides = [(ups[r], downs[r])]
            if halves == 2:
                sides.append(([swap(a, "ctx") for a in ups[r]], [swap(a, "ctx") for a in downs[r]]))
        for h, (up_pieces, down_pieces) in enumerate(sides):
            for kind, pieces in ((0, up_pieces), (1, down_pieces)):
                at = 0
                for piece in pieces:
                    unit.append((kind, h, at, piece))
                    at += piece.shape[0]
        units.append(unit)
    return units, halves


def weight_grads(x_all, u_all, act_all, dgu_all, halves, expert_parts, ctx_index):
    rows = (((0,), (0,)), ((), ()))
    hidden = act_all.shape[2]
    width = hidden // halves
    ups, downs = [None] * expert_parts, [None] * expert_parts
    for r in reversed(range(expert_parts)):

        def grads(h):
            d_up = lax.dot_general(
                x_all, dgu_all[r, :, h * 2 * width : (h + 1) * 2 * width], rows, preferred_element_type=jnp.float32
            )
            d_down = lax.dot_general(
                act_all[r, :, h * width : (h + 1) * width], u_all, rows, preferred_element_type=jnp.float32
            )
            return d_up, d_down

        if halves == 2:
            sent = [swap(low(g), "ctx") for g in grads(1)]
            up, down = [low(g + f32(s)) for g, s in zip(grads(0), sent)]
        else:
            up, down = [low(g) for g in grads(0)]
        ups[r], downs[r] = up, down
    up = low(cube_scatter_halves(ups, "expert", expert_parts))
    down = low(cube_scatter_halves(downs, "expert", expert_parts))
    if halves == 1:
        return f32(lax.psum(up, "ctx")), f32(lax.psum(down, "ctx"))
    up_other, down_other = swap(up, "ctx"), swap(down, "ctx")
    first = ctx_index == 0
    up0, up1 = jnp.where(first, up, up_other), jnp.where(first, up_other, up)
    down0, down1 = jnp.where(first, down, down_other), jnp.where(first, down_other, down)
    return (
        f32(jnp.concatenate([up0[:, :width], up1[:, :width], up0[:, width:], up1[:, width:]], axis=1)),
        f32(jnp.concatenate([down0, down1], axis=0)),
    )


def on_device(
    prompt_tokens,
    sequel_tokens,
    attention_gain,
    query_weight,
    key_weight,
    value_weight,
    query_gain,
    key_gain,
    out_weight,
    feed_gain,
    router_weight,
    gate_up_weight,
    down_weight,
    prompt_routes,
    sequel_routes,
    prompt_cotangent,
    sequel_cotangent,
):
    expert_parts, ctx_parts, dp_parts = (lax.axis_size(a) for a in ("expert", "ctx", "dp"))
    expert_index, ctx_index, dp_index = (lax.axis_index(a) for a in ("expert", "ctx", "dp"))
    prompt_rows = prompt_tokens.shape[1]
    sequel_rows = sequel_tokens.shape[2]
    rows = prompt_rows + 2 * sequel_rows
    share = rows // expert_parts
    model_width = prompt_tokens.shape[2]
    head_dim = query_gain.shape[0]
    query_width = query_weight.shape[1]
    query_heads = query_width // head_dim
    kv_first = expert_index * query_heads // (H // KV)
    experts = router_weight.shape[1]
    assert query_heads <= H // KV and gate_up_weight.shape[0] == 1
    prompt_total, sequel_total = prompt_rows * ctx_parts, sequel_rows * ctx_parts
    contract_rows = (((0,), (0,)), ((), ()))
    contract_cols = (((1,), (1,)), ((), ()))

    def stacked(prompt, sequel):
        return jnp.concatenate([prompt[0], sequel[0, 0], sequel[0, 1]], axis=0)

    def my_share(whole):
        return lax.dynamic_slice_in_dim(whole, expert_index * share, share, 0)

    units, halves = weight_units(
        gate_up_weight[0], down_weight[0], expert_parts, ctx_parts, ctx_index
    )
    upstream_mine = my_share(stacked(prompt_cotangent, sequel_cotangent))
    routes_mine = my_share(stacked(prompt_routes, sequel_routes))
    u_slots = ring_gather(upstream_mine, "dp", dp_parts)
    route_slots = ring_gather(routes_mine, "dp", dp_parts)

    tokens_low = stacked(prompt_tokens, sequel_tokens)
    hidden = low(rms_scaled(f32(tokens_low), attention_gain))
    qkv_weight = jnp.concatenate(
        [query_weight]
        + [
            lax.dynamic_slice_in_dim(w, kv_first * head_dim, head_dim, 1)
            for w in (key_weight, value_weight)
        ],
        axis=1,
    )
    pre = jnp.dot(hidden, qkv_weight, preferred_element_type=jnp.float32)
    key_pre = pre[:, query_width : query_width + head_dim]
    index_row = jnp.arange(rows, dtype=jnp.int32)
    position = jnp.where(
        index_row < prompt_rows,
        ctx_index * prompt_rows + index_row,
        prompt_total + ctx_index * sequel_rows + (index_row - prompt_rows) % sequel_rows,
    )
    cosine, sine = rotary_tables(f32(position), head_dim)
    key_local = low(turn(rms_scaled(key_pre, key_gain), cosine, sine))
    kv_local = jnp.concatenate([key_local, low(pre[:, query_width + head_dim :])], axis=1)
    kv_slots = ring_gather(kv_local, "ctx", ctx_parts)

    def spans(slot):
        owner = lax.rem(ctx_index - slot + ctx_parts, ctx_parts)
        return (
            (owner * prompt_rows, prompt_rows),
            (prompt_total + owner * sequel_rows, sequel_rows),
            (prompt_total + sequel_total + owner * sequel_rows, sequel_rows),
        )

    kv_all = jnp.zeros((rows * ctx_parts, 2 * head_dim), jnp.bfloat16)
    for s, block in enumerate(kv_slots):
        at = 0
        for first, size in spans(s):
            kv_all = lax.dynamic_update_slice_in_dim(kv_all, block[at : at + size], first, 0)
            at += size
    keys, values = kv_all[:, :head_dim], kv_all[:, head_dim:]
    own = ctx_index.reshape(1).astype(jnp.int32)
    query_gain_row = query_gain.reshape(1, head_dim)
    queries, heads, lse = attend(
        own, pre, query_gain_row, cosine, sine, keys, values, sequel_rows, prompt_total, query_heads
    )
    heads_cube = to_cube(heads, expert_index, expert_parts)
    partial = low(jnp.dot(heads_cube, out_weight, preferred_element_type=jnp.float32))
    attention_share = cube_scatter_halves(
        [partial[r * share : (r + 1) * share] for r in range(expert_parts)], "expert", expert_parts
    )
    tokens_mine = f32(my_share(tokens_low))
    residual = tokens_mine + attention_share
    normed = low(rms_scaled(residual, feed_gain))

    lane = jnp.arange(128, dtype=jnp.int32)
    lane_expert = jnp.where(
        lane < experts,
        (expert_index ^ (lane % expert_parts)) * dp_parts + (dp_index + lane // expert_parts) % dp_parts,
        -1,
    )
    lane_hot = (jnp.arange(experts, dtype=jnp.int32)[:, None] == lane_expert[None, :]).astype(jnp.bfloat16)
    router_lanes = low(jnp.dot(router_weight, lane_hot, preferred_element_type=jnp.float32))
    router_rows = router_lanes.T

    def gates_of(x, routes):
        logits = jnp.dot(x, router_lanes, preferred_element_type=jnp.float32)
        named = jnp.any(routes[:, :, None] == lane_expert[None, None, :], axis=1)
        peak = jnp.max(jnp.where(named, logits, -jnp.inf), axis=-1, keepdims=True)
        weights = jnp.where(named, jnp.exp(logits - peak), 0.0)
        return weights / jnp.sum(weights, axis=-1, keepdims=True)

    x_slots = ring_gather(normed, "dp", dp_parts)
    gate_slots = [gates_of(x, routes) for x, routes in zip(x_slots, route_slots)]
    mixes, row_parts, coefs = [], [], []
    kept = None
    for s in range(dp_parts):
        mix, row, coef, *kept = moe_rows(
            x_slots[s], u_slots[s], gate_slots[s], router_rows, units, halves, s, dp_parts, kept
        )
        mixes.append(mix)
        row_parts.append(row)
        coefs.append(coef)
    row_sum = ring_scatter(row_parts, "dp", dp_parts)
    dot = ring_scatter([jnp.sum(coef, axis=1) for coef in coefs], "dp", dp_parts)
    mixture = ring_scatter(mixes, "dp", dp_parts)
    layer_share = low(residual + mixture)
    gates = gate_slots[0]
    gates_dot = gates * dot[:, None]
    normed_grad = row_sum - jnp.dot(gates_dot, f32(router_rows), precision=HIGHEST)
    residual_part, feed_terms = rms_backward(residual, feed_gain, normed_grad)
    residual_grad = f32(upstream_mine) + residual_part
    feed_gain_grad = jnp.sum(feed_terms, axis=0)
    residual_cube = cube_gather_halves(low(residual_grad), "expert", expert_parts)
    x_all = jnp.concatenate(x_slots, axis=0)
    u_all = jnp.concatenate(u_slots, axis=0)
    coef_all = jnp.concatenate([coefs[0] - gates_dot] + coefs[1:], axis=0)
    router_grad = jnp.dot(
        lax.dot_general(f32(x_all), coef_all, contract_rows, precision=HIGHEST), f32(lane_hot).T, precision=HIGHEST
    )
    gate_up_grad, down_grad = weight_grads(
        x_all, u_all, kept[0], kept[1], halves, expert_parts, ctx_index
    )

    residual_low = jnp.concatenate([piece for pieces in residual_cube for piece in pieces], axis=0)
    heads_grad_cube = low(
        lax.dot_general(residual_low, out_weight, contract_cols, preferred_element_type=jnp.float32)
    )
    heads_grad = from_cube(
        [[heads_grad_cube[r * share : (r + 1) * share]] for r in range(expert_parts)], expert_index
    )
    out_weight_grad = lax.dot_general(
        heads_cube, residual_low, contract_rows, preferred_element_type=jnp.float32
    )
    query_low, key_grads, value_grads, query_gain_grad = attend_back(
        own, queries, keys, keys.T, values, lse, heads, heads_grad, pre, query_gain_row, cosine, sine,
        sequel_rows, prompt_total,
    )
    kv_grads = low(jnp.concatenate([key_grads * (1.0 / LOG2E), value_grads], axis=1))
    kv_sum = ring_scatter(
        [
            jnp.concatenate([lax.dynamic_slice_in_dim(kv_grads, a, n, 0) for a, n in spans(s)], axis=0)
            for s in range(ctx_parts)
        ],
        "ctx",
        ctx_parts,
    )
    key_turned = turn(kv_sum[:, :head_dim], cosine, -sine)
    key_pre_grad, key_terms = rms_backward(key_pre, key_gain, key_turned)
    key_gain_grad = jnp.sum(key_terms, axis=0)
    low_grads = jnp.concatenate([query_low, low(key_pre_grad), low(kv_sum[:, head_dim:])], axis=1)
    hidden_grad = low(
        lax.dot_general(
            to_cube(low_grads, expert_index, expert_parts), qkv_weight, contract_cols, preferred_element_type=jnp.float32
        )
    )
    hidden_grad_mine = cube_scatter_halves(
        [hidden_grad[r * share : (r + 1) * share] for r in range(expert_parts)], "expert", expert_parts
    )
    qkv_grad = lax.dot_general(hidden, low_grads, contract_rows, preferred_element_type=jnp.float32)
    input_part, attention_terms = rms_backward(tokens_mine, attention_gain, hidden_grad_mine)
    attention_gain_grad = jnp.sum(attention_terms, axis=0)
    input_share = low(residual_grad + input_part)

    out_total = f32(lax.psum(low(out_weight_grad), ("ctx", "dp")))
    qkv_total = lax.psum(low(qkv_grad), ("ctx", "dp"))
    query_total = f32(qkv_total[:, :query_width])
    kv_total = qkv_total[:, query_width:]
    if expert_parts == KV:
        kv_cube = cube_gather(kv_total, "expert", expert_parts, cube_bits(expert_parts))
    else:
        kv_cube = None
    kv_outs = []
    for part in range(2):
        whole = jnp.zeros((model_width, KV * head_dim), jnp.float32)
        cols = slice(part * head_dim, (part + 1) * head_dim)
        if kv_cube is not None:
            for r in range(expert_parts):
                whole = lax.dynamic_update_slice_in_dim(
                    whole, f32(kv_cube[r][:, cols]), (expert_index ^ r) * head_dim, 1
                )
        else:
            whole = lax.dynamic_update_slice_in_dim(whole, f32(kv_total[:, cols]), kv_first * head_dim, 1)
            whole = f32(lax.psum(low(whole), "expert"))
        kv_outs.append(whole)
    everywhere = ("expert", "ctx", "dp")
    router_total, feed_total = lax.psum((router_grad, feed_gain_grad), everywhere)
    attention_total, query_gain_total, key_gain_total = lax.psum(
        (attention_gain_grad, query_gain_grad.reshape(head_dim), key_gain_grad), everywhere
    )
    layer_full = from_cube(cube_gather_halves(layer_share, "expert", expert_parts), expert_index)
    input_full = from_cube(cube_gather_halves(input_share, "expert", expert_parts), expert_index)

    def split(whole):
        return (
            whole[:prompt_rows][None],
            whole[prompt_rows:].reshape(1, 2, sequel_rows, model_width),
        )

    return (
        *split(layer_full),
        *split(input_full),
        attention_total,
        query_total,
        kv_outs[0],
        kv_outs[1],
        query_gain_total,
        key_gain_total,
        out_total,
        feed_total,
        router_total,
        gate_up_grad[None],
        down_grad[None],
    )


def solution(mesh):
    placed = (
        P("dp", "ctx", None),
        P("dp", None, "ctx", None),
        P(),
        P(None, "expert"),
        P(),
        P(),
        P(),
        P(),
        P("expert", None),
        P(),
        P(),
        P(("expert", "dp"), None, None),
        P(("expert", "dp"), None, None),
        P("dp", "ctx", None),
        P("dp", None, "ctx", None),
        P("dp", "ctx", None),
        P("dp", None, "ctx", None),
    )
    return jax.shard_map(
        on_device,
        mesh=mesh,
        in_specs=placed,
        out_specs=(
            P("dp", "ctx", None),
            P("dp", None, "ctx", None),
            P("dp", "ctx", None),
            P("dp", None, "ctx", None),
            P(),
            P(None, "expert"),
            P(),
            P(),
            P(),
            P(),
            P("expert", None),
            P(),
            P(),
            P(("expert", "dp"), None, None),
            P(("expert", "dp"), None, None),
        ),
        check_vma=False,
    )
```

time: 2770 us -> 1110 us (0.40)
  waiting for transfers between devices: 1860 us -> 430 us
  matrix products: 414 us -> 159 us
  Pallas kernels: 0 us -> 168 us
  other arithmetic: 228 us -> 98.7 us
  local copies, waits for them, and re-layouts: 187 us -> 76.7 us
  starting transfers between devices: 21.9 us -> 109 us
    all_to_all x4 -> x0, waiting for transfers between devices: 1400 us -> none  [move_slots(): lax.all_to_all(slot_rows, ('expert', 'dp'), split_axis=0, concat_axis=0,...]
    ppermute x0 -> x99, waiting for transfers between devices: none -> 430 us  [the longest x24 182 us: cube_scatter(): lax.ppermute(low(held.pop(r)), axis, [(j, j ^ bit) for j in range(size)])]
    psum x4 -> x2, waiting for transfers between devices: 333 us -> 0.01 us  [the longest x1 0.01 us: on_device(): qkv_total = lax.psum(low(qkv_grad), ('ctx', 'dp'))]
    dot_general x27 -> x30, matrix products: 414 us -> 159 us  [the longest x8 63.4 us: grads(): lax.dot_general(x_all, dgu_all[r, :, h * 2 * width:(h + 1) * 2 * width],...]
    pallas_call x0 -> x6, Pallas kernels: none -> 168 us  [the longest x4 121 us: moe_rows(): pl.pallas_call(functools.partial(moe_kernel, n_units, halves, pieces), gr...]
    ppermute x0 -> x99, starting transfers between devices: none -> 109 us  [the longest x33 35.6 us: cube_gather(): lax.ppermute(held[r], axis, [(j, j ^ bit) for j in range(size)])]
    gather x2 -> x0, local copies, waits for them, and re-layouts: 101 us -> none  [the longest x1 50.4 us: on_device(): row_back[flat_routes, slot_rank]]
    all_gather x2 -> x0, waiting for transfers between devices: 87.2 us -> none  [the longest x1 47.1 us: on_device(): lax.all_gather(residual_grad.astype(jnp.bfloat16), 'expert', axis=0, tile...]
  transfers between devices with their start and end apart: 13 -> 101, of which waited for: 12 -> 40; matrix products, arithmetic and copies ran while one was open for 12% -> 28% of each run, Pallas kernels for 0% -> 15%
where the time goes in v1:
time: 1110 us; the launch traced here: 1100 us
  waiting for transfers between devices  430 us (39%)
  Pallas kernels  168 us (15%)
  matrix products  159 us (14%)
  starting transfers between devices  109 us (10%)
  other arithmetic  98.7 us (9%)
  local copies, waits for them, and re-layouts  76.7 us (7%)
  blocking collectives  42.8 us (4%)
  between operations  16.7 us (2%)
    ppermute x24, waiting for transfers between devices, cube_scatter(): lax.ppermute(low(held.pop(r)), axis, [(j, j ^ bit) for j in range(size)])  182 us
    ppermute x33, waiting for transfers between devices, cube_gather(): lax.ppermute(held[r], axis, [(j, j ^ bit) for j in range(size)])  149 us
    pallas_call x4, Pallas kernels, moe_rows(): pl.pallas_call(functools.partial(moe_kernel, n_units, halves, pieces), gr...  121 us
    ppermute x10, waiting for transfers between devices, ring_scatter(): lax.ppermute(total, axis, [(j, (j + 1) % size) for j in range(size)])  70.3 us
    dot_general x8, matrix products, grads(): lax.dot_general(x_all, dgu_all[r, :, h * 2 * width:(h + 1) * 2 * width],...  63.4 us
    psum x1, blocking collectives, on_device(): lax.psum((attention_gain_grad, query_gain_grad.reshape(head_dim), key_gai...  42.8 us
    dot_general x8, matrix products, grads(): lax.dot_general(act_all[r, :, h * width:(h + 1) * width], u_all, rows, pr...  36.8 us
    ppermute x33, starting transfers between devices, cube_gather(): lax.ppermute(held[r], axis, [(j, j ^ bit) for j in range(size)])  35.6 us
  transfers between devices with their start and end apart: 101, of which 40 were waited for; matrix products, arithmetic and copies ran while one was open for 28% of the time, Pallas kernels for 15%

profile of v1, /device:TPU:0, one launch (start us, length us, event | category | flops | bytes accessed | tf_op | source)
XLA Modules:
  0.0 1101.1 jit_solution(11942167367677423829)
XLA Ops:
  55.3 16.3 %shard_map.280 = (bf16[8,1024,128]{2,1,0:T(8,128)(2,1)S(1)}, bf16[1024,1024]{1,0:T(8,128)(2,1)S(1)}, f32[8,1024]{1,0:T(8,128)S(1)}) custom-call(s32[1]{0:T(128)} %bitcast.3.own_ref, f32[1024,1280]{1,0:T(8,128)S(1)} %copy-done.7, f32[1,128]{1,0:T(1,128)S(1)} %bitcast.118, f32[1024,128]{1,0:T(8,128)S(1)} %get-tuple-element.176.cos_ref, ...), custom_call_target="tpu_custom_call" | custom-call | flops 8589934592 | bytes 10485760 | tf_op jit(solution)/shard_map/pallas_call | solution.py:358
  117.2 10.7 collective-permute-done.4
  142.3 44.4 %collective-permute-done.6 = bf16[128,2048]{1,0:T(8,128)(2,1)S(1)} collective-permute-done((bf16[128,2048]{1,0:T(8,128)(2,1)S(1)}, bf16[128,2048]{1,0:T(8,128)(2,1)S(1)}, u32[]{:S(2)}, u32[]{:S(2)}) %collective-permute-start.6) | collective-permute-done | bytes 524320 | tf_op jit(solution)/shard_map/ppermute | solution.py:97
  193.9 12.7 %collective-permute-done.18.refs_16_ = bf16[1024,768]{1,0:T(8,128)(2,1)S(1)} collective-permute-done((bf16[1024,768]{1,0:T(8,128)(2,1)S(1)}, bf16[1024,768]{1,0:T(8,128)(2,1)S(1)}, u32[]{:S(2)}, u32[]{:S(2)}) %collective-permute-start.18) | collective-permute-done | bytes 1572896 | tf_op jit(solution)/shard_map/ppermute | solution.py:81
  207.8 15.6 %collective-permute-done.28.refs_26_ = bf16[192,2048]{1,0:T(8,128)(2,1)S(1)} collective-permute-done((bf16[192,2048]{1,0:T(8,128)(2,1)}, bf16[192,2048]{1,0:T(8,128)(2,1)S(1)}, u32[]{:S(2)}, u32[]{:S(2)}) %collective-permute-start.28) | collective-permute-done | bytes 786464 | tf_op jit(solution)/shard_map/ppermute | solution.py:81
  228.2 12.3 %collective-permute-start.7 = (bf16[256,2048]{1,0:T(8,128)(2,1)}, bf16[256,2048]{1,0:T(8,128)(2,1)}, u32[]{:S(2)}, u32[]{:S(2)}) collective-permute-start(bf16[256,2048]{1,0:T(8,128)(2,1)} %multiply_convert_fusion.refs_0_), channel_id=1, source_target_pairs={{0,1},{1,2},{2,3},{3,0},{4,5},{5,6},{6,7},{7,4},{8,9},{9,10},{10,1... | collective-permute-start | bytes 3145736 | tf_op jit(solution)/shard_map/ppermute | solution.py:57
  253.0 14.0 %collective-permute-done.7.refs_0_ = bf16[256,2048]{1,0:T(8,128)(2,1)} collective-permute-done((bf16[256,2048]{1,0:T(8,128)(2,1)}, bf16[256,2048]{1,0:T(8,128)(2,1)}, u32[]{:S(2)}, u32[]{:S(2)}) %collective-permute-start.7) | collective-permute-done | bytes 1048608 | tf_op jit(solution)/shard_map/ppermute | solution.py:57
  302.0 30.3 %shard_map.281 = (bf16[256,2048]{1,0:T(8,128)(2,1)}, bf16[256,2048]{1,0:T(8,128)(2,1)}, f32[256,128]{1,0:T(8,128)}, bf16[4,1024,768]{2,1,0:T(8,128)(2,1)}, bf16[4,1024,1536]{2,1,0:T(8,128)(2,1)}) custom-call(bf16[256,2048]{1,0:T(8,128)(2,1)} %multiply_convert_fusion.refs_0_, bf16[256,2048]{1,0:T(8,128)(2,1)} %copy-done.31, f32[256,128]{1,0:T(8,128)} %fusion.88.refs_2_, ...), custom_call_target="tpu_custom_call" | custom-call | flops 19327352832 | bytes 37748736 | tf_op jit(solution)/shard_map/pallas_call | solution.py:230
  332.3 30.3 %shard_map.282 = (bf16[256,2048]{1,0:T(8,128)(2,1)}, bf16[256,2048]{1,0:T(8,128)(2,1)}, f32[256,128]{1,0:T(8,128)}, bf16[4,1024,768]{2,1,0:T(8,128)(2,1)}, bf16[4,1024,1536]{2,1,0:T(8,128)(2,1)}) custom-call(bf16[256,2048]{1,0:T(8,128)(2,1)} %collective-permute-done.7.refs_0_, ...), custom_call_target="tpu_custom_call", output_to_operand_aliasing={{3}: (32, {}), {4}: (33, {})} | custom-call | flops 19327352832 | bytes 37748736 | tf_op jit(solution)/shard_map/pallas_call | solution.py:230
  369.0 30.3 %shard_map.283 = (bf16[256,2048]{1,0:T(8,128)(2,1)}, bf16[256,2048]{1,0:T(8,128)(2,1)}, f32[256,128]{1,0:T(8,128)}, bf16[4,1024,768]{2,1,0:T(8,128)(2,1)}, bf16[4,1024,1536]{2,1,0:T(8,128)(2,1)}) custom-call(bf16[256,2048]{1,0:T(8,128)(2,1)} %collective-permute-done.35.refs_0_, ...), custom_call_target="tpu_custom_call", output_to_operand_aliasing={{3}: (32, {}), {4}: (33, {})} | custom-call | flops 19327352832 | bytes 37748736 | tf_op jit(solution)/shard_map/pallas_call | solution.py:230
  403.4 30.3 %shard_map.284 = (bf16[256,2048]{1,0:T(8,128)(2,1)}, bf16[256,2048]{1,0:T(8,128)(2,1)}, f32[256,128]{1,0:T(8,128)}, bf16[4,1024,768]{2,1,0:T(8,128)(2,1)}, bf16[4,1024,1536]{2,1,0:T(8,128)(2,1)}) custom-call(bf16[256,2048]{1,0:T(8,128)(2,1)} %collective-permute-done.39.refs_0_, ...), custom_call_target="tpu_custom_call", output_to_operand_aliasing={{3}: (32, {}), {4}: (33, {})} | custom-call | flops 19327352832 | bytes 37748736 | tf_op jit(solution)/shard_map/pallas_call | solution.py:230
  449.2 15.7 %collective-permute-done.38 = bf16[256,2048]{1,0:T(8,128)(2,1)} collective-permute-done((bf16[256,2048]{1,0:T(8,128)(2,1)}, bf16[256,2048]{1,0:T(8,128)(2,1)}, u32[]{:S(2)}, u32[]{:S(2)}) %collective-permute-start.38) | collective-permute-done | bytes 1048608 | tf_op jit(solution)/shard_map/ppermute | solution.py:66
  467.4 20.0 %collective-permute-done.50 = bf16[256,2048]{1,0:T(8,128)(2,1)} collective-permute-done((bf16[256,2048]{1,0:T(8,128)(2,1)}, bf16[256,2048]{1,0:T(8,128)(2,1)}, u32[]{:S(2)}, u32[]{:S(2)}) %collective-permute-start.50) | collective-permute-done | bytes 1048608 | tf_op jit(solution)/shard_map/ppermute | solution.py:66
  496.0 13.8 %collective-permute-done.42 = bf16[256,2048]{1,0:T(8,128)(2,1)S(1)} collective-permute-done((bf16[256,2048]{1,0:T(8,128)(2,1)S(1)}, bf16[256,2048]{1,0:T(8,128)(2,1)S(1)}, u32[]{:S(2)}, u32[]{:S(2)}) %collective-permute-start.42) | collective-permute-done | bytes 1048608 | tf_op jit(solution)/shard_map/ppermute | solution.py:66
  509.8 20.8 %collective-permute-done.51 = bf16[256,2048]{1,0:T(8,128)(2,1)S(1)} collective-permute-done((bf16[256,2048]{1,0:T(8,128)(2,1)S(1)}, bf16[256,2048]{1,0:T(8,128)(2,1)S(1)}, u32[]{:S(2)}, u32[]{:S(2)}) %collective-permute-start.51) | collective-permute-done | bytes 1048608 | tf_op jit(solution)/shard_map/ppermute | solution.py:66
  582.8 30.7 %shard_map.285 = (bf16[1024,1024]{1,0:T(8,128)(2,1)S(1)}, f32[2048,128]{1,0:T(8,128)S(1)}, f32[2048,128]{1,0:T(8,128)S(1)}, f32[1,128]{1,0:T(1,128)S(1)}) custom-call(s32[1]{0:T(128)} %bitcast.3.own_ref, bf16[8,1024,128]{2,1,0:T(8,128)(2,1)S(1)} %copy-done.17, bf16[2048,128]{1,0:T(8,128)(2,1)S(1)} %copy-done.11, bf16[128,2048]{1,0:T(8,128)(2,1)S(1)} %copy.63.kt_ref, ...), custom_call_target="tpu_custom_call" | custom-call | flops 21474836480 | bytes 12582912 | tf_op jit(solution)/shard_map/pallas_call | solution.py:380
  613.9 11.9 %collective-permute-start.61 = (bf16[1024,256]{1,0:T(8,128)(2,1)S(1)}, bf16[1024,256]{1,0:T(8,128)(2,1)S(1)}, u32[]{:S(2)}, u32[]{:S(2)}) collective-permute-start(bf16[1024,256]{1,0:T(8,128)(2,1)S(1)} %pad_maximum_fusion.16), channel_id=1, source_target_pairs={{0,4},{4,0},{1,5},{5,1},{2,6},{6,2},{3,7},{7,3},{8,12},{12,8},{9,1... | collective-permute-start | bytes 1572872 | tf_op jit(solution)/shard_map/ppermute | solution.py:66
  796.9 40.4 %collective-permute-done.47 = bf16[128,2048]{1,0:T(8,128)(2,1)S(1)} collective-permute-done((bf16[128,2048]{1,0:T(8,128)(2,1)S(1)}, bf16[128,2048]{1,0:T(8,128)(2,1)S(1)}, u32[]{:S(2)}, u32[]{:S(2)}) %collective-permute-start.47) | collective-permute-done | bytes 524320 | tf_op jit(solution)/shard_map/ppermute | solution.py:81
  851.2 10.7 collective-permute-done.63
  896.5 33.8 %collective-permute-done.65 = bf16[128,2048]{1,0:T(8,128)(2,1)S(1)} collective-permute-done((bf16[128,2048]{1,0:T(8,128)(2,1)S(1)}, bf16[128,2048]{1,0:T(8,128)(2,1)S(1)}, u32[]{:S(2)}, u32[]{:S(2)}) %collective-permute-start.65) | collective-permute-done | bytes 524320 | tf_op jit(solution)/shard_map/ppermute | solution.py:97
  931.5 17.6 %collective-permute-done.67 = bf16[128,2048]{1,0:T(8,128)(2,1)S(1)} collective-permute-done((bf16[128,2048]{1,0:T(8,128)(2,1)S(1)}, bf16[128,2048]{1,0:T(8,128)(2,1)S(1)}, u32[]{:S(2)}, u32[]{:S(2)}) %collective-permute-start.67) | collective-permute-done | bytes 524320 | tf_op jit(solution)/shard_map/ppermute | solution.py:97
  955.8 42.8 %all-reduce = (f32[2048]{0:T(1024)}, f32[128]{0:T(128)}, f32[128]{0:T(128)}, f32[2048]{0:T(1024)}) all-reduce(f32[2048]{0:T(1024)S(1)} %get-tuple-element.71, f32[128]{0:T(128)S(1)} %bitcast.117, f32[128]{0:T(128)S(1)} %copy-done.86, f32[2048]{0:T(1024)S(1)} %copy-done.74), channel_id=1, replica_groups=mesh['expert'=4,'ctx'=2,'dp'=4] {'expert','ctx','dp'}, use_global_device_ids=true, to_apply=%region_24.25 | all-reduce | flops 4352 | bytes 34816 | tf_op jit(solution)/shard_map/psum | solution.py:683
  1011.4 15.0 %collective-permute-done.71 = bf16[128,2048]{1,0:T(8,128)(2,1)S(1)} collective-permute-done((bf16[128,2048]{1,0:T(8,128)(2,1)}, bf16[128,2048]{1,0:T(8,128)(2,1)S(1)}, u32[]{:S(2)}, u32[]{:S(2)}) %collective-permute-start.71) | collective-permute-done | bytes 524320 | tf_op jit(solution)/shard_map/ppermute | solution.py:81
  1076.7 14.1 %collective-permute-done.76 = bf16[2048,256]{1,0:T(8,128)(2,1)S(1)} collective-permute-done((bf16[2048,256]{1,0:T(8,128)(2,1)S(1)}, bf16[2048,256]{1,0:T(8,128)(2,1)S(1)}, u32[]{:S(2)}, u32[]{:S(2)}) %collective-permute-start.76) | collective-permute-done | bytes 1048608 | tf_op jit(solution)/shard_map/ppermute | solution.py:81
  (590 shorter events, 549.8 us)
Async XLA Ops:
  7.2 1034.7 %all-reduce.7.cloned.1.call-start = ((), (), s32[]{:S(2)}) async-start(), calls=%async_computation.1 | async-start | bytes 18874368 | tf_op jit(solution)/shard_map/psum | solution.py:661
  9.8 88.1 %collective-permute-start.21 = (bf16[192,2048]{1,0:T(8,128)(2,1)}, bf16[192,2048]{1,0:T(8,128)(2,1)}, u32[]{:S(2)}, u32[]{:S(2)}) collective-permute-start(bf16[192,2048]{1,0:T(8,128)(2,1)} %get-tuple-element.128), channel_id=1, source_target_pairs={{0,16},{8,24},{16,0},{24,8},{1,17},{9,25},{17,1},{25,9},{2,18},{10... | collective-permute-start | bytes 2359304 | tf_op jit(solution)/shard_map/ppermute | solution.py:81
  12.8 86.6 %collective-permute-start.13 = (bf16[192,2048]{1,0:T(8,128)(2,1)}, bf16[192,2048]{1,0:T(8,128)(2,1)}, u32[]{:S(2)}, u32[]{:S(2)}) collective-permute-start(bf16[192,2048]{1,0:T(8,128)(2,1)} %get-tuple-element.128), channel_id=1, source_target_pairs={{0,8},{8,0},{16,24},{24,16},{1,9},{9,1},{17,25},{25,17},{2,10},{10... | collective-permute-start | bytes 2359304 | tf_op jit(solution)/shard_map/ppermute | solution.py:81
  116.7 72.2 %collective-permute-start.19 = (bf16[1024,768]{1,0:T(8,128)(2,1)S(1)}, bf16[1024,768]{1,0:T(8,128)(2,1)S(1)}, u32[]{:S(2)}, u32[]{:S(2)}) collective-permute-start(bf16[1024,768]{1,0:T(8,128)(2,1)S(1)} %get-tuple-element.130), channel_id=1, source_target_pairs={{0,16},{8,24},{16,0},{24,8},{1,17},{9,25},{17,1},{25,9},{2,18},{10... | collective-permute-start | bytes 4718600 | tf_op jit(solution)/shard_map/ppermute | solution.py:81
  127.9 63.1 %collective-permute-start.11 = (bf16[1024,768]{1,0:T(8,128)(2,1)S(1)}, bf16[1024,768]{1,0:T(8,128)(2,1)S(1)}, u32[]{:S(2)}, u32[]{:S(2)}) collective-permute-start(bf16[1024,768]{1,0:T(8,128)(2,1)S(1)} %get-tuple-element.130), channel_id=1, source_target_pairs={{0,8},{8,0},{16,24},{24,16},{1,9},{9,1},{17,25},{25,17},{2,10},{10... | collective-permute-start | bytes 4718600 | tf_op jit(solution)/shard_map/ppermute | solution.py:81
  139.1 67.4 %collective-permute-start.18 = (bf16[1024,768]{1,0:T(8,128)(2,1)S(1)}, bf16[1024,768]{1,0:T(8,128)(2,1)S(1)}, u32[]{:S(2)}, u32[]{:S(2)}) collective-permute-start(bf16[1024,768]{1,0:T(8,128)(2,1)S(1)} %get-tuple-element.131), channel_id=1, source_target_pairs={{0,16},{8,24},{16,0},{24,8},{1,17},{9,25},{17,1},{25,9},{2,18},{10... | collective-permute-start | bytes 4718600 | tf_op jit(solution)/shard_map/ppermute | solution.py:81
  141.8 81.6 %collective-permute-start.28 = (bf16[192,2048]{1,0:T(8,128)(2,1)}, bf16[192,2048]{1,0:T(8,128)(2,1)S(1)}, u32[]{:S(2)}, u32[]{:S(2)}) collective-permute-start(bf16[192,2048]{1,0:T(8,128)(2,1)} %collective-permute-done.12.refs_10_), channel_id=1, source_target_pairs={{0,16},{8,24},{16,0},{24,8},{1,17},{9,25},{17,1},{25,9},{2,18},{10... | collective-permute-start | bytes 2359304 | tf_op jit(solution)/shard_map/ppermute | solution.py:81
  301.9 101.5 %collective-permute-start.40 = (bf16[256,2048]{1,0:T(8,128)(2,1)}, bf16[256,2048]{1,0:T(8,128)(2,1)}, u32[]{:S(2)}, u32[]{:S(2)}) collective-permute-start(bf16[256,2048]{1,0:T(8,128)(2,1)} %copy-done.94), channel_id=1, source_target_pairs={{0,1},{1,2},{2,3},{3,0},{4,5},{5,6},{6,7},{7,4},{8,9},{9,10},{10,1... | collective-permute-start | bytes 3145736 | tf_op jit(solution)/shard_map/ppermute | solution.py:57
  301.9 98.7 %collective-permute-start.39 = (bf16[256,2048]{1,0:T(8,128)(2,1)}, bf16[256,2048]{1,0:T(8,128)(2,1)}, u32[]{:S(2)}, u32[]{:S(2)}) collective-permute-start(bf16[256,2048]{1,0:T(8,128)(2,1)} %collective-permute-done.35.refs_0_), channel_id=1, source_target_pairs={{0,1},{1,2},{2,3},{3,0},{4,5},{5,6},{6,7},{7,4},{8,9},{9,10},{10,1... | collective-permute-start | bytes 3145736 | tf_op jit(solution)/shard_map/ppermute | solution.py:57
  364.4 69.4 %collective-permute-start.34 = (bf16[256,2048]{1,0:T(8,128)(2,1)}, bf16[256,2048]{1,0:T(8,128)(2,1)}, u32[]{:S(2)}, u32[]{:S(2)}) collective-permute-start(bf16[256,2048]{1,0:T(8,128)(2,1)} %get-tuple-element.45), channel_id=1, source_target_pairs={{0,1},{1,2},{2,3},{3,0},{4,5},{5,6},{6,7},{7,4},{8,9},{9,10},{10,1... | collective-permute-start | bytes 3145736 | tf_op jit(solution)/shard_map/ppermute | solution.py:66
  368.5 68.9 %collective-permute-start.49 = (bf16[256,2048]{1,0:T(8,128)(2,1)}, bf16[256,2048]{1,0:T(8,128)(2,1)}, u32[]{:S(2)}, u32[]{:S(2)}) collective-permute-start(bf16[256,2048]{1,0:T(8,128)(2,1)} %get-tuple-element.53), channel_id=1, source_target_pairs={{0,1},{1,2},{2,3},{3,0},{4,5},{5,6},{6,7},{7,4},{8,9},{9,10},{10,1... | collective-permute-start | bytes 3145736 | tf_op jit(solution)/shard_map/ppermute | solution.py:66
  448.9 243.3 %collective-permute-start.92 = (bf16[384,2048]{1,0:T(8,128)(2,1)}, bf16[384,2048]{1,0:T(8,128)(2,1)}, u32[]{:S(2)}, u32[]{:S(2)}) collective-permute-start(bf16[384,2048]{1,0:T(8,128)(2,1)} %convolution_convert_fusion.8), channel_id=1, source_target_pairs={{0,4},{4,0},{1,5},{5,1},{2,6},{6,2},{3,7},{7,3},{8,12},{12,8},{9,1... | collective-permute-start | bytes 4718600 | tf_op jit(solution)/shard_map/ppermute | solution.py:112
  551.0 146.6 %collective-permute-start.89 = (bf16[384,2048]{1,0:T(8,128)(2,1)}, bf16[384,2048]{1,0:T(8,128)(2,1)}, u32[]{:S(2)}, u32[]{:S(2)}) collective-permute-start(bf16[384,2048]{1,0:T(8,128)(2,1)} %convolution_convert_fusion.10), channel_id=1, source_target_pairs={{0,4},{4,0},{1,5},{5,1},{2,6},{6,2},{3,7},{7,3},{8,12},{12,8},{9,1... | collective-permute-start | bytes 4718600 | tf_op jit(solution)/shard_map/ppermute | solution.py:112
  560.3 141.8 %collective-permute-start.91 = (bf16[384,2048]{1,0:T(8,128)(2,1)}, bf16[384,2048]{1,0:T(8,128)(2,1)}, u32[]{:S(2)}, u32[]{:S(2)}) collective-permute-start(bf16[384,2048]{1,0:T(8,128)(2,1)} %convolution_convert_fusion.9), channel_id=1, source_target_pairs={{0,4},{4,0},{1,5},{5,1},{2,6},{6,2},{3,7},{7,3},{8,12},{12,8},{9,1... | collective-permute-start | bytes 4718600 | tf_op jit(solution)/shard_map/ppermute | solution.py:112
  644.9 447.3 %all-reduce.5.cloned.1.call-start = ((), (), s32[]{:S(2)}) async-start(), calls=%async_computation | async-start | bytes 262144 | tf_op jit(solution)/shard_map/psum | solution.py:682
  660.2 68.7 %collective-permute-start.78 = (bf16[2048,768]{1,0:T(8,128)(2,1)}, bf16[2048,768]{1,0:T(8,128)(2,1)}, u32[]{:S(2)}, u32[]{:S(2)}) collective-permute-start(bf16[2048,768]{1,0:T(8,128)(2,1)} %convolution_convert_fusion.6), channel_id=1, source_target_pairs={{0,4},{4,0},{1,5},{5,1},{2,6},{6,2},{3,7},{7,3},{8,12},{12,8},{9,1... | collective-permute-start | bytes 9437192 | tf_op jit(solution)/shard_map/ppermute | solution.py:112
  692.2 69.1 %collective-permute-start.81 = (bf16[2048,768]{1,0:T(8,128)(2,1)}, bf16[2048,768]{1,0:T(8,128)(2,1)}, u32[]{:S(2)}, u32[]{:S(2)}) collective-permute-start(bf16[2048,768]{1,0:T(8,128)(2,1)} %convolution_convert_fusion.4), channel_id=1, source_target_pairs={{0,4},{4,0},{1,5},{5,1},{2,6},{6,2},{3,7},{7,3},{8,12},{12,8},{9,1... | collective-permute-start | bytes 9437192 | tf_op jit(solution)/shard_map/ppermute | solution.py:112
  772.0 91.3 %collective-permute-start.85 = (bf16[1024,768]{1,0:T(8,128)(2,1)}, bf16[1024,768]{1,0:T(8,128)(2,1)}, u32[]{:S(2)}, u32[]{:S(2)}) collective-permute-start(bf16[1024,768]{1,0:T(8,128)(2,1)} %get-tuple-element.127), channel_id=1, source_target_pairs={{0,16},{8,24},{16,0},{24,8},{1,17},{9,25},{17,1},{25,9},{2,18},{10... | collective-permute-start | bytes 4718600 | tf_op jit(solution)/shard_map/ppermute | solution.py:97
  781.8 85.4 %collective-permute-start.82 = (bf16[1024,768]{1,0:T(8,128)(2,1)}, bf16[1024,768]{1,0:T(8,128)(2,1)}, u32[]{:S(2)}, u32[]{:S(2)}) collective-permute-start(bf16[1024,768]{1,0:T(8,128)(2,1)} %get-tuple-element.126), channel_id=1, source_target_pairs={{0,8},{8,0},{16,24},{24,16},{1,9},{9,1},{17,25},{25,17},{2,10},{10... | collective-permute-start | bytes 4718600 | tf_op jit(solution)/shard_map/ppermute | solution.py:97
  796.9 92.4 %collective-permute-start.98 = (bf16[384,2048]{1,0:T(8,128)(2,1)}, bf16[384,2048]{1,0:T(8,128)(2,1)}, u32[]{:S(2)}, u32[]{:S(2)}) collective-permute-start(bf16[384,2048]{1,0:T(8,128)(2,1)} %pad_maximum_fusion.12), channel_id=1, source_target_pairs={{0,4},{4,0},{1,5},{5,1},{2,6},{6,2},{3,7},{7,3},{8,12},{12,8},{9,1... | collective-permute-start | bytes 4718600 | tf_op jit(solution)/shard_map/ppermute | solution.py:112
  867.1 132.3 %collective-permute-start.79 = (bf16[1024,768]{1,0:T(8,128)(2,1)}, bf16[1024,768]{1,0:T(8,128)(2,1)S(1)}, u32[]{:S(2)}, u32[]{:S(2)}) collective-permute-start(bf16[1024,768]{1,0:T(8,128)(2,1)} %slice.511), channel_id=1, source_target_pairs={{0,8},{8,0},{16,24},{24,16},{1,9},{9,1},{17,25},{25,17},{2,10},{10... | collective-permute-start | bytes 4718600 | tf_op jit(solution)/shard_map/ppermute | solution.py:97
  873.2 129.0 %collective-permute-start.84 = (bf16[1024,768]{1,0:T(8,128)(2,1)}, bf16[1024,768]{1,0:T(8,128)(2,1)}, u32[]{:S(2)}, u32[]{:S(2)}) collective-permute-start(bf16[1024,768]{1,0:T(8,128)(2,1)} %slice.515), channel_id=1, source_target_pairs={{0,16},{8,24},{16,0},{24,8},{1,17},{9,25},{17,1},{25,9},{2,18},{10... | collective-permute-start | bytes 4718600 | tf_op jit(solution)/shard_map/ppermute | solution.py:97
  888.2 114.5 %collective-permute-start.86 = (bf16[1024,768]{1,0:T(8,128)(2,1)}, bf16[1024,768]{1,0:T(8,128)(2,1)}, u32[]{:S(2)}, u32[]{:S(2)}) collective-permute-start(bf16[1024,768]{1,0:T(8,128)(2,1)} %add_convert_fusion.9), channel_id=1, source_target_pairs={{0,8},{8,0},{16,24},{24,16},{1,9},{9,1},{17,25},{25,17},{2,10},{10... | collective-permute-start | bytes 4718600 | tf_op jit(solution)/shard_map/ppermute | solution.py:97
  930.3 73.5 %collective-permute-start.83 = (bf16[1024,768]{1,0:T(8,128)(2,1)}, bf16[1024,768]{1,0:T(8,128)(2,1)}, u32[]{:S(2)}, u32[]{:S(2)}) collective-permute-start(bf16[1024,768]{1,0:T(8,128)(2,1)} %add_convert_fusion.12), channel_id=1, source_target_pairs={{0,16},{8,24},{16,0},{24,8},{1,17},{9,25},{17,1},{25,9},{2,18},{10... | collective-permute-start | bytes 4718600 | tf_op jit(solution)/shard_map/ppermute | solution.py:97
  (180 other events, 4032.5 us)
Sparse Core Ops, SparseCore 0:
  645.1 194.4 all-reduce.6
  845.7 123.1 all-reduce.4

commit v2 on v1

v2 whole, which is shorter than its diff:
```python
import functools
import math

import jax
import jax.numpy as jnp
from jax import lax
from jax.experimental import pallas as pl
from jax.experimental.pallas import tpu as pltpu
from jax.sharding import PartitionSpec as P

H = 32
KV = 4
P_SIZE = 1024


NORM_EPS = 1e-06
ROPE_BASE = 1000000.0
HIGHEST = lax.Precision.HIGHEST
LOG2E = math.log2(math.e)


def rms_scaled(values, gain_row):
    return (
        values * lax.rsqrt(jnp.mean(values * values, axis=-1, keepdims=True) + NORM_EPS) * gain_row
    )


def rms_backward(values, gain_row, upstream):
    inverse = lax.rsqrt(jnp.mean(values * values, axis=-1, keepdims=True) + NORM_EPS)
    unit_rows = values * inverse
    scaled = upstream * gain_row
    inner_mean = jnp.mean(scaled * unit_rows, axis=-1, keepdims=True)
    return (inverse * (scaled - unit_rows * inner_mean), upstream * unit_rows)


def rotary_tables(positions, head_width):
    halfway = head_width // 2
    frequency = jnp.exp(
        jnp.arange(halfway, dtype=jnp.float32) * (-2.0 * math.log(ROPE_BASE) / head_width)
    )
    angles = positions[:, None] * frequency[None, :]
    cosine, sine = jnp.cos(angles), jnp.sin(angles)
    return (jnp.concatenate([cosine, cosine], 1), jnp.concatenate([-sine, sine], 1))


def f32(values):
    return values.astype(jnp.float32)


def low(values):
    return values.astype(jnp.bfloat16)


def ring_gather(own, axis, size):
    held = [own]
    for _ in range(size - 1):
        held.append(lax.ppermute(held[-1], axis, [(j, (j + 1) % size) for j in range(size)]))
    return held


def ring_scatter(parts, axis, size):
    if size == 1:
        return f32(parts[0])
    total = parts[1]
    for s in range(2, size + 1):
        total = lax.ppermute(total, axis, [(j, (j + 1) % size) for j in range(size)])
        total = f32(total) + f32(parts[s % size])
        if s < size:
            total = total.astype(parts[0].dtype)
    return total


def cube_bits(size):
    return [1 << k for k in range(size.bit_length() - 1)]


def cube_gather(own, axis, size, bits):
    held = {0: own}
    for bit in bits:
        for r in list(held):
            held[r ^ bit] = lax.ppermute(held[r], axis, [(j, j ^ bit) for j in range(size)])
    return [held[r] for r in range(size)]


def cube_scatter(parts, axis, size, bits):
    held = dict(enumerate(parts))
    for bit in bits:
        for r in [r for r in held if r & bit]:
            there = lax.ppermute(low(held.pop(r)), axis, [(j, j ^ bit) for j in range(size)])
            total = f32(held[r ^ bit]) + f32(there)
            held[r ^ bit] = total if bit == bits[-1] else low(total)
    return f32(held[0])


def plane_hop(values, second):
    return lax.ppermute(
        values, ("expert", "ctx"), [(2 * j + c, 2 * (j ^ (1 if c == second else 2)) + c) for j in range(4) for c in range(2)]
    )


def plane_gather(own, quick, size):
    if not quick:
        return cube_gather(own, "expert", size, cube_bits(size))
    near = plane_hop(own, 0)
    return [own, near, plane_hop(own, 1), plane_hop(near, 1)]


def plane_scatter(blocks, quick, size, *hold):
    share = blocks.shape[0] // size
    if not quick:
        return cube_scatter(
            [blocks[r * share : (r + 1) * share] for r in range(size)], "expert", size, cube_bits(size)
        ), blocks
    came = plane_hop(blocks[2 * share :], 1)
    near = low(f32(blocks[share : 2 * share]) + f32(came[share:]))
    if hold:
        near = after(near, *hold)
    return f32(blocks[:share]) + f32(came[:share]) + f32(plane_hop(near, 0)), near


def sign(values):
    return values[:16, :128]


def after(value, *others):
    others = [sign(o) for o in others]
    anywhere = pl.BlockSpec(memory_space=pl.ANY)
    return pl.pallas_call(
        lambda *refs: None,
        in_specs=[anywhere] * (1 + len(others)),
        out_specs=anywhere,
        out_shape=jax.ShapeDtypeStruct(value.shape, value.dtype),
        input_output_aliases={0: 0},
    )(value, *others)


def butterfly(values, axes):
    for axis in axes:
        size = lax.axis_size(axis)
        for bit in cube_bits(size):
            values = values + lax.ppermute(values, axis, [(j, j ^ bit) for j in range(size)])
    return values


def swap(values, axis):
    return lax.ppermute(values, axis, [(0, 1), (1, 0)])


def to_slots(rows, order):
    share = rows.shape[0] // len(order)
    return jnp.concatenate([lax.dynamic_slice_in_dim(rows, at * share, share, 0) for at in order], axis=0)


def from_slots(rows, order):
    share = rows.shape[0] // len(order)
    whole = jnp.zeros_like(rows)
    for u, at in enumerate(order):
        whole = lax.dynamic_update_slice_in_dim(whole, rows[u * share : (u + 1) * share], at * share, 0)
    return whole


def dot_nn(a, b):
    return lax.dot_general(a, b, (((1,), (0,)), ((), ())), preferred_element_type=jnp.float32)


def dot_nt(a, b):
    return lax.dot_general(a, b, (((1,), (1,)), ((), ())), preferred_element_type=jnp.float32)


def moe_kernel(n_units, pieces, turned, half_ref, *refs):
    n_w = sum(len(p) for p in pieces)
    x_ref, u_ref, gates_ref, router_ref = refs[:4]
    w_refs = refs[4 : 4 + n_w]
    mix_ref, row_ref, coef_ref, act_ref, dgu_ref = refs[-11 - turned : -6 - turned]
    gu_buf, d_buf, mix_acc, row_acc, gg_acc, sems = refs[-6:]
    unit = pl.program_id(0)
    hidden = act_ref.shape[2]

    def copies(k, slot):
        base = sum(len(p) for p in pieces[:k])
        out = []
        for j, (kind, off, size) in enumerate(pieces[k]):
            if isinstance(off, str):
                off = pl.multiple_of((half_ref[0] if off == "mine" else 1 - half_ref[0]) * size, size)
            buf = d_buf if kind else gu_buf
            out.append(pltpu.make_async_copy(w_refs[base + j], buf.at[slot, pl.ds(off, size)], sems.at[slot, j]))
        return out

    @pl.when(unit == 0)
    def _():
        for c in copies(0, 0):
            c.start()
        mix_acc[...] = jnp.zeros_like(mix_acc)
        row_acc[...] = jnp.zeros_like(row_acc)
        gg_acc[...] = jnp.zeros_like(gg_acc)
        if turned:
            refs[-7][...] = x_ref[...].T

    for k in range(n_units):

        @pl.when(unit == k)
        def _(k=k):
            if k + 1 < n_units:
                for c in copies(k + 1, (k + 1) % 2):
                    c.start()
            for c in copies(k, k % 2):
                c.wait()

    slot = lax.rem(unit, 2)
    gates = gates_ref[...]
    lane = lax.broadcasted_iota(jnp.int32, gates.shape, 1)
    here = lane == unit
    gate = jnp.sum(jnp.where(here, gates, 0.0), axis=1, keepdims=True)
    gu = gu_buf[slot]
    down = d_buf[slot]
    back = dot_nt(u_ref[...], down)
    pre = dot_nn(x_ref[...], gu)
    g_part = pre[:, :hidden]
    u_part = pre[:, hidden:]
    sig = 1.0 / (1.0 + jnp.exp(-g_part))
    silu = g_part * sig
    active = silu * u_part
    act = (active * gate).astype(jnp.bfloat16)
    act_ref[0] = act
    gg_acc[...] += jnp.where(here, jnp.sum(active * back, axis=1, keepdims=True), 0.0)
    ag = back * gate
    dg = (ag * u_part * (sig + silu * (1.0 - sig))).astype(jnp.bfloat16)
    dgu = jnp.concatenate([dg, (ag * silu).astype(jnp.bfloat16)], axis=1)
    dgu_ref[0] = dgu
    mix_acc[...] += dot_nn(act, down)
    row_acc[...] += dot_nt(dgu, gu)

    @pl.when(unit == n_units - 1)
    def _():
        coef = gates * gg_acc[...]
        coef = coef - gates * jnp.sum(coef, axis=1, keepdims=True)
        coef_ref[...] = coef
        mix_ref[...] = mix_acc[...].astype(jnp.bfloat16)
        extra = dot_nn(coef.astype(jnp.bfloat16), router_ref[...])
        row_ref[...] = (row_acc[...] + extra).astype(jnp.bfloat16)


def moe_rows(places, x, u, gates, router_rows, units, slots, kept, others):
    rows, width = x.shape
    n_units = len(units)
    pieces = [[(k, o, a.shape[0]) for k, o, a in unit] for unit in units]
    arrays = [a for unit in units for _, _, a in unit]
    hidden = arrays[0].shape[1] // 2
    most = max(len(p) for p in pieces)
    anywhere = pl.BlockSpec(memory_space=pl.ANY)
    turned = int(rows % 128 == 0)

    def whole(shape):
        return pl.BlockSpec(shape, lambda i, s: (0,) * len(shape))

    others = [sign(o) for o in others]
    operands = [places, x, u, gates, router_rows] + arrays + others
    in_specs = [whole(x.shape), pl.BlockSpec((rows, width), lambda i, s: (0, 0))]
    in_specs += [whole(gates.shape), whole(router_rows.shape)]
    in_specs += [anywhere] * (len(arrays) + len(others))
    aliases = {}
    if kept is not None:
        aliases = {len(operands) + k: 3 + k for k in range(len(kept))}
        in_specs += [anywhere] * len(kept)
        operands += list(kept)
    return pl.pallas_call(
        functools.partial(moe_kernel, n_units, pieces, turned),
        grid_spec=pltpu.PrefetchScalarGridSpec(
            num_scalar_prefetch=1,
            grid=(n_units,),
            in_specs=in_specs,
            out_specs=[
                whole((rows, width)),
                whole((rows, width)),
                whole((rows, 128)),
                pl.BlockSpec((1, rows, hidden), lambda i, s: (i, s[1], 0)),
                pl.BlockSpec((1, rows, 2 * hidden), lambda i, s: (i, s[1], 0)),
                pl.BlockSpec((width, rows), lambda i, s: (0, s[1])),
            ][: 5 + turned],
            scratch_shapes=[
                pltpu.VMEM((2, width, 2 * hidden), jnp.bfloat16),
                pltpu.VMEM((2, hidden, width), jnp.bfloat16),
                pltpu.VMEM((rows, width), jnp.float32),
                pltpu.VMEM((rows, width), jnp.float32),
                pltpu.VMEM((rows, 128), jnp.float32),
                pltpu.SemaphoreType.DMA((2, most)),
            ],
        ),
        out_shape=[
            jax.ShapeDtypeStruct((rows, width), jnp.bfloat16),
            jax.ShapeDtypeStruct((rows, width), jnp.bfloat16),
            jax.ShapeDtypeStruct((rows, 128), jnp.float32),
            jax.ShapeDtypeStruct((n_units, slots * rows, hidden), jnp.bfloat16),
            jax.ShapeDtypeStruct((n_units, slots * rows, 2 * hidden), jnp.bfloat16),
            jax.ShapeDtypeStruct((width, slots * rows), jnp.bfloat16),
        ][: 5 + turned],
        input_output_aliases=aliases,
        compiler_params=pltpu.CompilerParams(
            vmem_limit_bytes=56 * 1024 * 1024, dimension_semantics=("arbitrary",)
        ),
        cost_estimate=pl.CostEstimate(
            flops=2 * rows * width * hidden * 6 * n_units,
            bytes_accessed=sum(a.size * 2 for a in arrays),
            transcendentals=rows * hidden * n_units,
        ),
    )(*operands)


def grad_kernel(width, with_sum, core_ref, *refs):
    xt_ref, ut_ref, dgu_ref, act_ref = refs[:4]
    out_ref = refs[-1]
    up = dot_nn(xt_ref[...], dgu_ref[0])
    down = dot_nn(ut_ref[...], act_ref[0])
    if with_sum:
        up = up + refs[4][:, : 2 * width].astype(jnp.float32)
        down = down + refs[4][:, 2 * width :].astype(jnp.float32)
    out_ref[:, : 2 * width] = up.astype(jnp.bfloat16)
    out_ref[:, 2 * width :] = down.astype(jnp.bfloat16)


def packed_grads(core, xt, ut, dgu, act, unit, other_half, added, others):
    model, rows = xt.shape
    width = act.shape[2]
    tile = min(512, model // 2)
    tiles = model // 2 // tile
    others = [sign(o) for o in others]
    operands = [core, xt, ut, dgu, act] + ([added] if added is not None else []) + others
    row = pl.BlockSpec((tile, rows), lambda i, s: (((1 - s[0]) if other_half else s[0]) * tiles + i, 0))
    packed = pl.BlockSpec((tile, 3 * width), lambda i, s: (i, 0))
    return pl.pallas_call(
        functools.partial(grad_kernel, width, added is not None),
        grid_spec=pltpu.PrefetchScalarGridSpec(
            num_scalar_prefetch=1,
            grid=(tiles,),
            in_specs=[
                row,
                row,
                pl.BlockSpec((1, rows, 2 * width), lambda i, s: (unit, 0, 0)),
                pl.BlockSpec((1, rows, width), lambda i, s: (unit, 0, 0)),
            ]
            + ([packed] if added is not None else [])
            + [pl.BlockSpec(memory_space=pl.ANY)] * len(others),
            out_specs=packed,
        ),
        out_shape=jax.ShapeDtypeStruct((model // 2, 3 * width), jnp.bfloat16),
        compiler_params=pltpu.CompilerParams(
            vmem_limit_bytes=48 * 1024 * 1024, dimension_semantics=("arbitrary",)
        ),
        cost_estimate=pl.CostEstimate(
            flops=rows * model * 3 * width, bytes_accessed=model * rows * 2 + model * width * 3, transcendentals=0
        ),
    )(*operands)


def key_row(t, block, prompt_blocks, segment, segment_rows):
    later = prompt_blocks * block + segment * segment_rows + (t - prompt_blocks) * block
    return pl.multiple_of(jnp.where(t < prompt_blocks, t * block, later), block)

def block_plan(own, block, prompt_blocks, own_prompt):
    at = pl.program_id(0)
    is_prompt = at < own_prompt
    full = jnp.where(is_prompt, own * own_prompt + at, prompt_blocks + own)
    return full, jnp.maximum(at - own_prompt, 0)

def turn(values, cosine, sine):
    half = values.shape[-1] // 2
    return values * cosine + jnp.concatenate([values[:, half:], values[:, :half]], axis=-1) * sine

def fwd_kernel(heads, block, prompt_blocks, own_prompt, segment_rows, scale,
               own_ref, pre_ref, gain_ref, cos_ref, sin_ref, k_ref, v_ref, *rest):
    q_ref, out_ref, lse_ref, acc = rest[-4:]
    full, segment = block_plan(own_ref[0], block, prompt_blocks, own_prompt)
    width = k_ref.shape[1]
    cosine, sine, gain = cos_ref[...], sin_ref[...], gain_ref[...]
    for h in range(heads):
        pre = pre_ref[:, h * width:(h + 1) * width]
        unit = pre * lax.rsqrt(jnp.mean(pre * pre, axis=1, keepdims=True) + NORM_EPS) * gain
        q_ref[h] = (turn(unit, cosine, sine) * scale).astype(jnp.bfloat16)
    acc[...] = jnp.zeros_like(acc)

    def step(t, masked):
        first = key_row(t, block, prompt_blocks, segment, segment_rows)
        keys = k_ref[pl.ds(first, block)]
        values = jnp.concatenate([v_ref[pl.ds(first, block)], jnp.ones((block, width), jnp.bfloat16)], axis=1)
        for h in range(heads):
            p = jnp.exp2(dot_nt(q_ref[h], keys))
            if masked:
                p = jnp.where(lax.broadcasted_iota(jnp.int32, p.shape, 1) <= lax.broadcasted_iota(jnp.int32, p.shape, 0), p, 0.0)
            acc[h] += dot_nn(p.astype(jnp.bfloat16), values)

    @pl.loop(0, full)
    def _(t):
        step(t, False)
    step(full, True)
    for h in range(heads):
        total = acc[h, :, width:]
        out_ref[:, h * width:(h + 1) * width] = (acc[h, :, :width] / total).astype(jnp.bfloat16)
        lse_ref[h:h + 1] = jnp.log2(total).T[:1]

def bwd_kernel(heads, block, prompt_blocks, own_prompt, segment_rows, scale,
               own_ref, q_ref, k_ref, kt_ref, v_ref, lse_ref, out_ref, do_ref, pre_ref, gain_ref, cos_ref, sin_ref, *rest):
    dpre_ref, dk_ref, dv_ref, dgain_ref, acc, delta = rest[-6:]
    full, segment = block_plan(own_ref[0], block, prompt_blocks, own_prompt)
    width = k_ref.shape[1]

    @pl.when(pl.program_id(0) == 0)
    def _():
        dk_ref[...] = jnp.zeros_like(dk_ref)
        dv_ref[...] = jnp.zeros_like(dv_ref)
        dgain_ref[...] = jnp.zeros_like(dgain_ref)

    for h in range(heads):
        cols = slice(h * width, (h + 1) * width)
        prod = out_ref[:, cols].astype(jnp.float32) * do_ref[:, cols].astype(jnp.float32)
        delta[h:h + 1] = jnp.sum(prod.T, axis=0, keepdims=True)
    acc[...] = jnp.zeros_like(acc)

    def step(t, masked):
        first = key_row(t, block, prompt_blocks, segment, segment_rows)
        rows = pl.ds(first, block)
        keys = k_ref[rows]
        kt = kt_ref[:, rows]
        values = v_ref[rows]
        dk = dv = 0.0
        for h in range(heads):
            q = q_ref[h]
            do = do_ref[:, h * width:(h + 1) * width]
            p = jnp.exp2(dot_nt(keys, q) - lse_ref[h:h + 1])
            if masked:
                p = jnp.where(lax.broadcasted_iota(jnp.int32, p.shape, 0) <= lax.broadcasted_iota(jnp.int32, p.shape, 1), p, 0.0)
            ds = (p * (dot_nt(values, do) - delta[h:h + 1])).astype(jnp.bfloat16)
            dv += dot_nn(p.astype(jnp.bfloat16), do)
            dk += dot_nn(ds, q)
            acc[h] += dot_nn(kt, ds)
        dk_ref[rows] += dk
        dv_ref[rows] += dv

    @pl.loop(0, full)
    def _(t):
        step(t, False)
    step(full, True)
    cosine, sine, gain = cos_ref[...], sin_ref[...], gain_ref[...]
    dgain = 0.0
    for h in range(heads):
        cols = slice(h * width, (h + 1) * width)
        turned = turn(acc[h].T * scale, cosine, -sine)
        pre = pre_ref[:, cols]
        inverse = lax.rsqrt(jnp.mean(pre * pre, axis=1, keepdims=True) + NORM_EPS)
        unit = pre * inverse
        scaled = turned * gain
        dpre_ref[:, cols] = (inverse * (scaled - unit * jnp.mean(scaled * unit, axis=1, keepdims=True))).astype(jnp.bfloat16)
        dgain = dgain + jnp.sum(turned * unit, axis=0, keepdims=True)
    dgain_ref[...] += dgain

def attend(own, pre, gain, cosine, sine, keys, values, block, prompt_total, heads, others):
    rows = pre.shape[0]
    head = keys.shape[1]
    width = heads * head
    own_prompt = rows // block - 2
    segment_rows = (keys.shape[0] - prompt_total) // 2
    scale = LOG2E / math.sqrt(head)
    whole = lambda shape: pl.BlockSpec(shape, lambda i, s: (0,) * len(shape))
    row = lambda w: pl.BlockSpec((block, w), lambda i, s: (i, 0))
    moved = lambda w: pl.BlockSpec((block, w), lambda i, s: (s[1 + i], 0))
    return pl.pallas_call(
        functools.partial(fwd_kernel, heads, block, prompt_total // block, own_prompt, segment_rows, scale),
        grid_spec=pltpu.PrefetchScalarGridSpec(
            num_scalar_prefetch=1, grid=(rows // block,),
            in_specs=[row(width), whole((1, head)), row(head), row(head), whole(keys.shape), whole(values.shape)]
                     + [pl.BlockSpec(memory_space=pl.ANY)] * len(others),
            out_specs=[pl.BlockSpec((heads, block, head), lambda i, s: (0, i, 0)), moved(width),
                       pl.BlockSpec((heads, block), lambda i, s: (0, i))],
            scratch_shapes=[pltpu.VMEM((heads, block, 2 * head), jnp.float32)]),
        out_shape=[jax.ShapeDtypeStruct((heads, rows, head), jnp.bfloat16), jax.ShapeDtypeStruct((rows, width), jnp.bfloat16),
                   jax.ShapeDtypeStruct((heads, rows), jnp.float32)],
        compiler_params=pltpu.CompilerParams(vmem_limit_bytes=40 * 1024 * 1024, dimension_semantics=("arbitrary",)),
        cost_estimate=pl.CostEstimate(flops=2 * rows * keys.shape[0] * width * 2, bytes_accessed=rows * width * 10, transcendentals=rows * keys.shape[0] * heads // 2),
    )(own, pre, gain, cosine, sine, keys, values, *[sign(o) for o in others])

def attend_back(own, q, keys, keys_t, values, lse, out, dout, pre, gain, cosine, sine, block, prompt_total, others):
    rows, width = out.shape
    head = keys.shape[1]
    heads = width // head
    own_prompt = rows // block - 2
    segment_rows = (keys.shape[0] - prompt_total) // 2
    whole = lambda shape: pl.BlockSpec(shape, lambda i, s: (0,) * len(shape))
    row = lambda w: pl.BlockSpec((block, w), lambda i, s: (i, 0))
    moved = lambda w: pl.BlockSpec((block, w), lambda i, s: (s[1 + i], 0))
    return pl.pallas_call(
        functools.partial(bwd_kernel, heads, block, prompt_total // block, own_prompt, segment_rows, 1.0 / math.sqrt(head)),
        grid_spec=pltpu.PrefetchScalarGridSpec(
            num_scalar_prefetch=1, grid=(rows // block,),
            in_specs=[pl.BlockSpec((heads, block, head), lambda i, s: (0, i, 0)), whole(keys.shape), whole(keys_t.shape), whole(values.shape),
                      pl.BlockSpec((heads, block), lambda i, s: (0, i)), moved(width), moved(width), row(width), whole((1, head)), row(head), row(head)]
                     + [pl.BlockSpec(memory_space=pl.ANY)] * len(others),
            out_specs=[row(width), whole(keys.shape), whole(keys.shape), whole((1, head))],
            scratch_shapes=[pltpu.VMEM((heads, head, block), jnp.float32), pltpu.VMEM((heads, block), jnp.float32)]),
        out_shape=[jax.ShapeDtypeStruct((rows, width), jnp.bfloat16), jax.ShapeDtypeStruct(keys.shape, jnp.float32),
                   jax.ShapeDtypeStruct(keys.shape, jnp.float32), jax.ShapeDtypeStruct((1, head), jnp.float32)],
        compiler_params=pltpu.CompilerParams(vmem_limit_bytes=40 * 1024 * 1024, dimension_semantics=("arbitrary",)),
        cost_estimate=pl.CostEstimate(flops=2 * rows * keys.shape[0] * width * 5, bytes_accessed=rows * width * 12, transcendentals=rows * keys.shape[0] * heads // 2),
    )(own, q, keys, keys_t, values, lse, out, dout, pre, gain, cosine, sine, *[sign(o) for o in others])


def plane_units(near, far, near_down, gate_up, down, ctx_index, hold):
    far_down = after(swap(near_down, "ctx"), hold)
    mine = [
        plane_hop(lax.dynamic_slice_in_dim(w, ctx_index * (w.shape[0] // 2), w.shape[0] // 2, 0), 0)
        for w in (far, far_down)
    ]
    return [
        [(0, 0, gate_up), (1, 0, down)],
        [(0, 0, near), (1, 0, near_down)],
        [(0, 0, far), (1, 0, far_down)],
        [(k, "mine", w) for k, w in enumerate(mine)] + [(k, "other", swap(w, "ctx")) for k, w in enumerate(mine)],
    ]


def unpack_kernel(core_ref, a_ref, b_ref, up_ref, down_ref):
    total = a_ref[...].astype(jnp.float32) + b_ref[...].astype(jnp.float32)
    width = total.shape[1] // 3
    up_ref[0] = total[:, : 2 * width]
    down_ref[0] = total[:, 2 * width :].T


def unpacked(core, own, came, half, outs):
    rows, packed = own.shape
    width = packed // 3
    tile = min(256, rows)
    tiles = rows // tile

    def at(i, s):
        return (s[0] if half == 0 else 1 - s[0]) * tiles + i

    anywhere = pl.BlockSpec(memory_space=pl.ANY)
    block = pl.BlockSpec((tile, packed), lambda i, s: (i, 0))
    return pl.pallas_call(
        (lambda c, a, b, *refs: unpack_kernel(c, a, b, *refs[-2:])),
        grid_spec=pltpu.PrefetchScalarGridSpec(
            num_scalar_prefetch=1,
            grid=(tiles,),
            in_specs=[block, block] + [anywhere] * len(outs),
            out_specs=[
                pl.BlockSpec((1, tile, 2 * width), lambda i, s: (0, at(i, s), 0)),
                pl.BlockSpec((1, width, tile), lambda i, s: (0, 0, at(i, s))),
            ],
        ),
        out_shape=[
            jax.ShapeDtypeStruct((1, 2 * rows, 2 * width), jnp.float32),
            jax.ShapeDtypeStruct((1, width, 2 * rows), jnp.float32),
        ],
        input_output_aliases={3 + k: k for k in range(len(outs))},
        compiler_params=pltpu.CompilerParams(
            vmem_limit_bytes=40 * 1024 * 1024, dimension_semantics=("arbitrary",)
        ),
        cost_estimate=pl.CostEstimate(flops=rows * packed, bytes_accessed=rows * packed * 8, transcendentals=0),
    )(core, own, came, *outs)


def place_kernel(order_ref, *refs):
    prompt_ref, sequel_ref = refs[-2:]
    at = pl.program_id(0)
    slot = order_ref[at]
    for u in range(4):

        @pl.when((slot == u) & (at < 2))
        def _(u=u):
            prompt_ref[0] = refs[u][...]

        @pl.when((slot == u) & (at >= 2))
        def _(u=u):
            sequel_ref[0, 0] = refs[u][...]


def place_rows(pieces, quick, order, slot_of, prompt_rows, sequel_rows):
    width = pieces[0].shape[1]
    if not quick:
        whole = from_slots(jnp.concatenate(pieces, axis=0), order)
        return whole[:prompt_rows][None], whole[prompt_rows:].reshape(1, 2, sequel_rows, width)
    share = pieces[0].shape[0]
    first = pl.BlockSpec((share, width), lambda i, s: (0, 0))
    return pl.pallas_call(
        place_kernel,
        grid_spec=pltpu.PrefetchScalarGridSpec(
            num_scalar_prefetch=1,
            grid=(4,),
            in_specs=[first] * 4,
            out_specs=[
                pl.BlockSpec((1, share, width), lambda i, s: (0, jnp.minimum(i, 1), 0)),
                pl.BlockSpec((1, 1, share, width), lambda i, s: (0, jnp.maximum(i - 2, 0), 0, 0)),
            ],
        ),
        out_shape=[
            jax.ShapeDtypeStruct((1, prompt_rows, width), pieces[0].dtype),
            jax.ShapeDtypeStruct((1, 2, sequel_rows, width), pieces[0].dtype),
        ],
        compiler_params=pltpu.CompilerParams(dimension_semantics=("arbitrary",)),
        cost_estimate=pl.CostEstimate(flops=0, bytes_accessed=16 * share * width, transcendentals=0),
    )(slot_of, *pieces)


def core_half(values, ctx_index):
    half = values.shape[0] // 2
    mine, other = (lax.dynamic_slice_in_dim(values, c * half, half, 0) for c in (ctx_index, 1 - ctx_index))
    return low(f32(mine) + f32(swap(other, "ctx")))


def both_halves(mine, ctx_index):
    other = swap(mine, "ctx")
    return jnp.concatenate(
        [jnp.where(ctx_index == 0, mine, other), jnp.where(ctx_index == 0, other, mine)], axis=0
    )


def on_device(
    prompt_tokens,
    sequel_tokens,
    attention_gain,
    query_weight,
    key_weight,
    value_weight,
    query_gain,
    key_gain,
    out_weight,
    feed_gain,
    router_weight,
    gate_up_weight,
    down_weight,
    prompt_routes,
    sequel_routes,
    prompt_cotangent,
    sequel_cotangent,
):
    expert_parts, ctx_parts, dp_parts = (lax.axis_size(a) for a in ("expert", "ctx", "dp"))
    expert_index, ctx_index, dp_index = (lax.axis_index(a) for a in ("expert", "ctx", "dp"))
    prompt_rows = prompt_tokens.shape[1]
    sequel_rows = sequel_tokens.shape[2]
    rows = prompt_rows + 2 * sequel_rows
    share = rows // expert_parts
    model_width = prompt_tokens.shape[2]
    head_dim = query_gain.shape[0]
    query_width = query_weight.shape[1]
    query_heads = query_width // head_dim
    kv_first = expert_index * query_heads // (H // KV)
    experts = router_weight.shape[1]
    assert query_heads <= H // KV and gate_up_weight.shape[0] == 1
    prompt_total, sequel_total = prompt_rows * ctx_parts, sequel_rows * ctx_parts
    contract_rows = (((0,), (0,)), ((), ()))
    contract_cols = (((1,), (1,)), ((), ()))

    def stacked(prompt, sequel):
        return jnp.concatenate([prompt[0], sequel[0, 0], sequel[0, 1]], axis=0)

    def my_share(whole):
        return lax.dynamic_slice_in_dim(whole, expert_index * share, share, 0)

    quick = expert_parts == 4 and ctx_parts == 2 and share == sequel_rows

    def turn_of(u):
        return jnp.where(ctx_index == 1, (u & 1) * 2 + (u >> 1), u) if quick else u

    order = [expert_index ^ turn_of(u) for u in range(expert_parts)]
    core = ctx_index.reshape(1).astype(jnp.int32)
    core = core if ctx_parts == 2 else 0 * core

    if quick:
        near_down = plane_hop(down_weight[0], 0)
        near_gate_up = plane_hop(gate_up_weight[0], 0)
    else:
        gathered = [cube_gather(w[0], "expert", expert_parts, cube_bits(expert_parts)) for w in (gate_up_weight, down_weight)]
        units = [[(0, 0, a), (1, 0, b)] for a, b in zip(*gathered)]
    tokens_low = stacked(prompt_tokens, sequel_tokens)
    hidden = low(rms_scaled(f32(tokens_low), attention_gain))
    upstream_mine = my_share(stacked(prompt_cotangent, sequel_cotangent))
    routes_mine = my_share(stacked(prompt_routes, sequel_routes))
    choices = routes_mine.shape[1]
    u_packed = jnp.concatenate([upstream_mine, jnp.pad(low(routes_mine), ((0, 0), (0, 128 - choices)))], axis=1)
    u_slots = ring_gather(after(u_packed, hidden), "dp", dp_parts)
    owners = [lax.rem(dp_index - s + dp_parts, dp_parts) for s in range(dp_parts)]

    qkv_weight = jnp.concatenate(
        [query_weight]
        + [
            lax.dynamic_slice_in_dim(w, kv_first * head_dim, head_dim, 1)
            for w in (key_weight, value_weight)
        ],
        axis=1,
    )
    pre = jnp.dot(hidden, qkv_weight, preferred_element_type=jnp.float32)
    key_pre = pre[:, query_width : query_width + head_dim]
    index_row = jnp.arange(rows, dtype=jnp.int32)
    position = jnp.where(
        index_row < prompt_rows,
        ctx_index * prompt_rows + index_row,
        prompt_total + ctx_index * sequel_rows + (index_row - prompt_rows) % sequel_rows,
    )
    cosine, sine = rotary_tables(f32(position), head_dim)
    key_local = low(turn(rms_scaled(key_pre, key_gain), cosine, sine))
    kv_local = jnp.concatenate([key_local, low(pre[:, query_width + head_dim :])], axis=1)
    if quick:
        kv_local = after(kv_local, u_slots[1])
    kv_slots = ring_gather(kv_local, "ctx", ctx_parts)

    def spans(slot):
        owner = lax.rem(ctx_index - slot + ctx_parts, ctx_parts)
        return (
            (owner * prompt_rows, prompt_rows),
            (prompt_total + owner * sequel_rows, sequel_rows),
            (prompt_total + sequel_total + owner * sequel_rows, sequel_rows),
        )

    kv_all = jnp.zeros((rows * ctx_parts, 2 * head_dim), jnp.bfloat16)
    for s, block in enumerate(kv_slots):
        at = 0
        for first, size in spans(s):
            kv_all = lax.dynamic_update_slice_in_dim(kv_all, block[at : at + size], first, 0)
            at += size
    keys, values = kv_all[:, :head_dim], kv_all[:, head_dim:]
    slot_of = jnp.stack([turn_of(expert_index ^ j) for j in range(expert_parts)]).astype(jnp.int32)
    storage = slot_of if quick else jnp.arange(rows // sequel_rows, dtype=jnp.int32)
    own = jnp.concatenate([ctx_index.reshape(1).astype(jnp.int32), storage])
    query_gain_row = query_gain.reshape(1, head_dim)
    queries, heads, lse = attend(
        own, pre, query_gain_row, cosine, sine, keys, values, sequel_rows, prompt_total, query_heads, []
    )
    heads_slots = heads if quick else to_slots(heads, order)
    partial = low(jnp.dot(heads_slots, out_weight, preferred_element_type=jnp.float32))
    if quick:
        partial = after(partial, near_gate_up, near_down, u_slots[2])
    attention_share, unused = plane_scatter(partial, quick, expert_parts, *u_slots[3:])
    tokens_mine = f32(my_share(tokens_low))
    residual = tokens_mine + attention_share
    normed = low(rms_scaled(residual, feed_gain))
    route_slots = [u[:, model_width : model_width + choices].astype(jnp.int32) for u in u_slots]

    lane = jnp.arange(128, dtype=jnp.int32)
    lane_expert = jnp.where(
        lane < experts,
        (expert_index ^ turn_of(lane % expert_parts)) * dp_parts + (dp_index + lane // expert_parts) % dp_parts,
        -1,
    )
    lane_hot = (jnp.arange(experts, dtype=jnp.int32)[:, None] == lane_expert[None, :]).astype(jnp.bfloat16)
    router_lanes = low(jnp.dot(router_weight, lane_hot, preferred_element_type=jnp.float32))
    router_rows = router_lanes.T

    def gates_of(x, routes):
        logits = jnp.dot(x, router_lanes, preferred_element_type=jnp.float32)
        named = jnp.any(routes[:, :, None] == lane_expert[None, None, :], axis=1)
        peak = jnp.max(jnp.where(named, logits, -jnp.inf), axis=-1, keepdims=True)
        weights = jnp.where(named, jnp.exp(logits - peak), 0.0)
        return weights / jnp.sum(weights, axis=-1, keepdims=True)

    def onward(total):
        return lax.ppermute(total, "dp", [(j, (j + 1) % dp_parts) for j in range(dp_parts)])

    x_slots = [normed]
    for _ in range(dp_parts - 1):
        x_slots.append(onward(x_slots[-1]))
    if quick:
        near_gate_up = after(near_gate_up, heads)
        far_gate_up = after(swap(near_gate_up, "ctx"), normed)
        units = plane_units(near_gate_up, far_gate_up, near_down, gate_up_weight[0], down_weight[0], ctx_index, x_slots[1])
    def rows_of(s, kept, others):
        return moe_rows(
            jnp.concatenate([core, owners[s].reshape(1).astype(jnp.int32)]),
            x_slots[s], u_slots[s], gates_of(x_slots[s], route_slots[s]), router_rows, units, dp_parts, kept, others,
        )

    mixes, coefs = ([None] * dp_parts for _ in range(2))
    kept, others, row_sum = None, [], None
    for s in [*range(1, dp_parts), 0]:
        mixes[s], row, coefs[s], *kept = rows_of(s, kept, others)
        if row_sum is not None:
            row = f32(row) + f32(onward(row_sum))
        row_sum = low(row) if s else f32(row)
        others = [row_sum] if s > 1 else []
    act_all, dgu_all = kept[:2]
    xt_all = kept[2] if len(kept) == 3 else from_slots(jnp.concatenate(x_slots, axis=0), owners).T
    u_all = after(jnp.concatenate([u[:, :model_width] for u in u_slots], axis=0), row_sum)
    ut_all = from_slots(u_all, owners).T

    def expert_grads(unit, other_half, added, *others):
        return packed_grads(core, xt_all, ut_all, dgu_all, act_all, unit, other_half, added, others)

    normed_grad = row_sum
    residual_part, feed_terms = rms_backward(residual, feed_gain, normed_grad)
    residual_grad = f32(upstream_mine) + residual_part
    feed_gain_grad = jnp.sum(feed_terms, axis=0)
    residual_mine = low(residual_grad)
    mix_sums = [after(mixes[1], residual_mine)]
    for s in range(2, dp_parts):
        mix_sums.append(low(f32(onward(mix_sums[-1])) + f32(mixes[s])))
    layer_share = low(residual + f32(onward(mix_sums[-1])) + f32(mixes[0]))

    residual_pieces = plane_gather(residual_mine, quick, expert_parts)
    residual_low = jnp.concatenate(residual_pieces, axis=0)

    if quick:
        far3 = expert_grads(3, True, None, residual_mine)
        far2 = expert_grads(2, True, None, far3, residual_pieces[1])
        near3 = expert_grads(3, False, swap(far3, "ctx"), far2)
        near1 = expert_grads(1, False, swap(far2, "ctx"), near3, mix_sums[1])
        diagonal, first = plane_hop(near3, 0), plane_hop(near1, 0)
        last = near1
    else:
        plane_grads = [
            jnp.concatenate([expert_grads(r, h, None, residual_mine) for h in (False, True)], axis=0)
            for r in range(expert_parts)
        ]
        last = plane_grads[-1]

    heads_grad_slots = low(
        lax.dot_general(residual_low, out_weight, contract_cols, preferred_element_type=jnp.float32)
    )
    heads_grad = heads_grad_slots if quick else from_slots(heads_grad_slots, order)
    out_weight_grad = lax.dot_general(
        heads_slots, residual_low, contract_rows, preferred_element_type=jnp.float32
    )
    out_weight_grad = low(out_weight_grad)
    if ctx_parts == 2:
        out_half = core_half(out_weight_grad, ctx_index)
    query_low, key_grads, value_grads, query_gain_grad = attend_back(
        own, queries, keys, keys.T, values, lse, heads, heads_grad, pre, query_gain_row, cosine, sine,
        sequel_rows, prompt_total, [last, out_weight_grad],
    )
    if quick:
        near2 = expert_grads(2, False, diagonal, query_low, mix_sums[2])
        near0 = expert_grads(0, False, first, near2, layer_share)
        key_grads = after(key_grads, diagonal)
    else:
        own_grads = lax.psum(
            low(cube_scatter(plane_grads, "expert", expert_parts, cube_bits(expert_parts))), "ctx"
        )
        width = down_weight.shape[1]
        gate_up_grad, down_grad = f32(own_grads[:, : 2 * width])[None], f32(own_grads[:, 2 * width :].T)[None]
        layer_pieces = plane_gather(layer_share, quick, expert_parts)
    coef_all = from_slots(
        after(jnp.concatenate(coefs, axis=0), query_low), owners
    )
    router_grad = jnp.dot(
        jnp.dot(f32(xt_all), coef_all, precision=HIGHEST), f32(lane_hot).T, precision=HIGHEST
    )
    kv_grads = low(jnp.concatenate([key_grads * (1.0 / LOG2E), value_grads], axis=1))
    kv_sum = ring_scatter(
        [
            jnp.concatenate([lax.dynamic_slice_in_dim(kv_grads, a, n, 0) for a, n in spans(s)], axis=0)
            for s in range(ctx_parts)
        ],
        "ctx",
        ctx_parts,
    )
    key_turned = turn(kv_sum[:, :head_dim], cosine, -sine)
    key_pre_grad, key_terms = rms_backward(key_pre, key_gain, key_turned)
    key_gain_grad = jnp.sum(key_terms, axis=0)
    low_grads = jnp.concatenate([query_low, low(key_pre_grad), low(kv_sum[:, head_dim:])], axis=1)
    hidden_grad = low(
        lax.dot_general(
            to_slots(low_grads, order), qkv_weight, contract_cols, preferred_element_type=jnp.float32
        )
    )
    hidden_grad_mine, hidden_near = plane_scatter(hidden_grad, quick, expert_parts, *([near0] if quick else []))
    if quick:
        far1 = expert_grads(1, True, swap(near2, "ctx"), hidden_near)
        layer_pieces = plane_gather(after(layer_share, hidden_grad_mine), quick, expert_parts)
        far0 = expert_grads(0, True, plane_hop(far1, 0))
        expert_outs = unpacked(core, near0, swap(far0, "ctx"), 0, [])
        gate_up_grad, down_grad = unpacked(core, far0, swap(near0, "ctx"), 1, expert_outs)
    query_grad = lax.dot_general(hidden, query_low, contract_rows, preferred_element_type=jnp.float32)
    kv_grad = lax.dot_general(hidden, low_grads[:, query_width:], contract_rows, preferred_element_type=jnp.float32)
    input_part, attention_terms = rms_backward(tokens_mine, attention_gain, hidden_grad_mine)
    attention_gain_grad = jnp.sum(attention_terms, axis=0)
    input_share = low(residual_grad + input_part)

    query_grad, kv_grad = low(query_grad), low(kv_grad)
    if ctx_parts == 2:
        halves = (out_half, core_half(query_grad, ctx_index), core_half(kv_grad, ctx_index))
        out_half, query_half, kv_half = lax.psum(halves, "dp")
        out_total, query_total = (f32(both_halves(h, ctx_index)) for h in (out_half, query_half))
    else:
        out_total, query_total = (f32(lax.psum(g, ("ctx", "dp"))) for g in (out_weight_grad, query_grad))
    if quick:
        half = model_width // 2
        kv_slots = jnp.concatenate(plane_gather(kv_half, quick, expert_parts), axis=0)
        kv_half = jnp.concatenate(
            [
                lax.dynamic_slice(kv_slots, (slot_of[j] * half, part * head_dim), (half, head_dim))
                for part in range(2)
                for j in range(KV)
            ],
            axis=1,
        )
        kv_whole = both_halves(kv_half, ctx_index)
        kv_outs = [f32(kv_whole[:, : KV * head_dim]), f32(kv_whole[:, KV * head_dim :])]
    else:
        kv_total = lax.psum(kv_grad, ("ctx", "dp"))
        kv_outs = []
        for part in range(2):
            whole = lax.dynamic_update_slice_in_dim(
                jnp.zeros((model_width, KV * head_dim), jnp.bfloat16),
                kv_total[:, part * head_dim : (part + 1) * head_dim],
                kv_first * head_dim,
                1,
            )
            kv_outs.append(f32(lax.psum(whole, "expert")))
    everywhere = ("ctx", "expert", "dp")
    smalls = [router_grad, feed_gain_grad, attention_gain_grad, query_gain_grad, key_gain_grad]
    small = jnp.concatenate([g.reshape(-1, 128) for g in smalls], axis=0)
    totals = butterfly(after(small, far0) if quick else small, everywhere)
    small_totals, at = [], 0
    for g in smalls:
        small_totals.append(totals[at : at + g.size // 128].reshape(g.shape))
        at += g.size // 128
    router_total, feed_total, attention_total, query_gain_total, key_gain_total = small_totals
    layer_out, input_out = (
        place_rows(pieces, quick, order, slot_of, prompt_rows, sequel_rows)
        for pieces in (layer_pieces, plane_gather(input_share, quick, expert_parts))
    )
    return (
        *layer_out,
        *input_out,
        attention_total,
        query_total,
        kv_outs[0],
        kv_outs[1],
        query_gain_total.reshape(head_dim),
        key_gain_total,
        out_total,
        feed_total,
        router_total,
        gate_up_grad,
        down_grad,
    )


def solution(mesh):
    placed = (
        P("dp", "ctx", None),
        P("dp", None, "ctx", None),
        P(),
        P(None, "expert"),
        P(),
        P(),
        P(),
        P(),
        P("expert", None),
        P(),
        P(),
        P(("expert", "dp"), None, None),
        P(("expert", "dp"), None, None),
        P("dp", "ctx", None),
        P("dp", None, "ctx", None),
        P("dp", "ctx", None),
        P("dp", None, "ctx", None),
    )
    return jax.shard_map(
        on_device,
        mesh=mesh,
        in_specs=placed,
        out_specs=(
            P("dp", "ctx", None),
            P("dp", None, "ctx", None),
            P("dp", "ctx", None),
            P("dp", None, "ctx", None),
            P(),
            P(None, "expert"),
            P(),
            P(),
            P(),
            P(),
            P("expert", None),
            P(),
            P(),
            P(("expert", "dp"), None, None),
            P(("expert", "dp"), None, None),
        ),
        check_vma=False,
    )
```

time: 1110 us -> 946 us (0.85)
  Pallas kernels: 168 us -> 281 us
  waiting for transfers between devices: 430 us -> 323 us
  matrix products: 159 us -> 61.5 us
  starting transfers between devices: 109 us -> 60.6 us
  blocking collectives: 42.8 us -> 0 us
  local copies, waits for them, and re-layouts: 76.7 us -> 105 us
    ppermute x57 -> x37, waiting for transfers between devices: 331 us -> 196 us  [the longest x23 117 us: plane_hop(): lax.ppermute(values, ('expert', 'ctx'), [(2 * j + c, 2 * (j ^ (1 if c ==...]
    pallas_call x4 -> x30, Pallas kernels: 121 us -> 232 us  [the longest x4 125 us: moe_rows(): pl.pallas_call(functools.partial(moe_kernel, n_units, pieces, turned), gr...]
    dot_general x23 -> x7, matrix products: 137 us -> 36.6 us  [the longest x1 8.25 us: on_device(): jnp.dot(heads_slots, out_weight, preferred_element_type=jnp.float32)]
    psum x2 -> x1, waiting for transfers between devices: 0.01 us -> 73 us  [on_device(): out_half, query_half, kv_half = lax.psum(halves, 'dp')]
    ppermute x10 -> x1, waiting for transfers between devices: 70.3 us -> 0.01 us  [ring_scatter(): lax.ppermute(total, axis, [(j, (j + 1) % size) for j in range(size)])]
    psum x1 -> x0, blocking collectives: 42.8 us -> none  [on_device(): lax.psum((attention_gain_grad, query_gain_grad.reshape(head_dim), key_gai...]
    ppermute x10 -> x4, waiting for transfers between devices: 28 us -> 53.1 us  [ring_gather(): lax.ppermute(held[-1], axis, [(j, (j + 1) % size) for j in range(size)])]
    convert_element_type x10 -> x17, other arithmetic: 11.7 us -> 35.1 us  [low(): return values.astype(jnp.bfloat16)]
  transfers between devices with their start and end apart: 101 -> 58, of which waited for: 40 -> 22; matrix products, arithmetic and copies ran while one was open for 28% -> 22% of each run, Pallas kernels for 15% -> 26%
where the time goes in v2:
time: 946 us; the launch traced here: 940 us
  waiting for transfers between devices  323 us (34%)
  Pallas kernels  281 us (30%)
  local copies, waits for them, and re-layouts  105 us (11%)
  other arithmetic  94.4 us (10%)
  matrix products  61.5 us (7%)
  starting transfers between devices  60.6 us (6%)
  between operations  16.1 us (2%)
    pallas_call x4, Pallas kernels, moe_rows(): pl.pallas_call(functools.partial(moe_kernel, n_units, pieces, turned), gr...  125 us
    ppermute x23, waiting for transfers between devices, plane_hop(): lax.ppermute(values, ('expert', 'ctx'), [(2 * j + c, 2 * (j ^ (1 if c ==...  117 us
    pallas_call x8, Pallas kernels, packed_grads(): pl.pallas_call(functools.partial(grad_kernel, width, added is not None),...  80.1 us
    psum x1, waiting for transfers between devices, on_device(): out_half, query_half, kv_half = lax.psum(halves, 'dp')  73 us
    ppermute x9, waiting for transfers between devices, onward(): lax.ppermute(total, 'dp', [(j, (j + 1) % dp_parts) for j in range(dp_part...  70.7 us
    ppermute x4, waiting for transfers between devices, ring_gather(): lax.ppermute(held[-1], axis, [(j, (j + 1) % size) for j in range(size)])  53.1 us
    unnamed x230, local copies, waits for them, and re-layouts  43.5 us
    convert_element_type x17, other arithmetic, low(): return values.astype(jnp.bfloat16)  35.1 us
  transfers between devices with their start and end apart: 58, of which 22 were waited for; matrix products, arithmetic and copies ran while one was open for 22% of the time, Pallas kernels for 26%

profile of v2, /device:TPU:0, one launch (start us, length us, event | category | flops | bytes accessed | tf_op | source)
XLA Modules:
  0.0 940.2 jit_solution(15135107424777294645)
XLA Ops:
  60.0 16.9 %shard_map.282 = (bf16[8,1024,128]{2,1,0:T(8,128)(2,1)S(1)}, bf16[1024,1024]{1,0:T(8,128)(2,1)S(1)}, f32[8,1024]{1,0:T(8,128)S(1)}) custom-call(s32[5]{0:T(128)S(1)} %concatenate.93.own_ref, f32[1024,1280]{1,0:T(8,128)S(1)} %copy-done.11, f32[1,128]{1,0:T(1,128)S(1)} %bitcast.63, f32[1024,128]{1,0:T(8,128)S(1)} %get-tuple-element.207.cos_ref, ...), custom_call_target="tpu_custom_call" | custom-call | flops 8589934592 | bytes 10485760 | tf_op jit(solution)/shard_map/pallas_call | solution.py:465
  94.2 20.2 %collective-permute-done.4.refs_1_ = bf16[256,2176]{1,0:T(8,128)(2,1)S(1)} collective-permute-done((bf16[256,2176]{1,0:T(8,128)(2,1)}, bf16[256,2176]{1,0:T(8,128)(2,1)S(1)}, u32[]{:S(2)}, u32[]{:S(2)}) %collective-permute-start.4) | collective-permute-done | bytes 1114144 | tf_op jit(solution)/shard_map/ppermute | solution.py:57
  120.0 27.8 %collective-permute-done.6.refs_1_ = bf16[256,2176]{1,0:T(8,128)(2,1)S(1)} collective-permute-done((bf16[256,2176]{1,0:T(8,128)(2,1)S(1)}, bf16[256,2176]{1,0:T(8,128)(2,1)S(1)}, u32[]{:S(2)}, u32[]{:S(2)}) %collective-permute-start.6) | collective-permute-done | bytes 1114144 | tf_op jit(solution)/shard_map/ppermute | solution.py:57
  153.8 14.5 %collective-permute-done.7 = bf16[256,2048]{1,0:T(8,128)(2,1)S(1)} collective-permute-done((bf16[256,2048]{1,0:T(8,128)(2,1)}, bf16[256,2048]{1,0:T(8,128)(2,1)S(1)}, u32[]{:S(2)}, u32[]{:S(2)}) %collective-permute-start.7) | collective-permute-done | bytes 1048608 | tf_op jit(solution)/shard_map/ppermute | solution.py:96
  188.7 19.2 %collective-permute-done.8.refs_0_ = bf16[256,2048]{1,0:T(8,128)(2,1)S(1)} collective-permute-done((bf16[256,2048]{1,0:T(8,128)(2,1)S(1)}, bf16[256,2048]{1,0:T(8,128)(2,1)S(1)}, u32[]{:S(2)}, u32[]{:S(2)}) %collective-permute-start.8) | collective-permute-done | bytes 1048608 | tf_op jit(solution)/shard_map/ppermute | solution.py:754
  222.1 23.0 %collective-permute-done.15.refs_0_ = bf16[256,2048]{1,0:T(8,128)(2,1)} collective-permute-done((bf16[256,2048]{1,0:T(8,128)(2,1)}, bf16[256,2048]{1,0:T(8,128)(2,1)}, u32[]{:S(2)}, u32[]{:S(2)}) %collective-permute-start.15) | collective-permute-done | bytes 1048608 | tf_op jit(solution)/shard_map/ppermute | solution.py:754
  249.6 23.0 %collective-permute-done.16.refs_0_ = bf16[256,2048]{1,0:T(8,128)(2,1)} collective-permute-done((bf16[256,2048]{1,0:T(8,128)(2,1)}, bf16[256,2048]{1,0:T(8,128)(2,1)}, u32[]{:S(2)}, u32[]{:S(2)}) %collective-permute-start.16) | collective-permute-done | bytes 1048608 | tf_op jit(solution)/shard_map/ppermute | solution.py:754
  275.4 31.3 %shard_map.288 = (bf16[256,2048]{1,0:T(8,128)(2,1)}, bf16[256,2048]{1,0:T(8,128)(2,1)}, f32[256,128]{1,0:T(8,128)}, bf16[4,1024,768]{2,1,0:T(8,128)(2,1)}, bf16[...) custom-call(s32[2]{0:T(128)} %pad_add_fusion.1.half_ref, bf16[256,2048]{1,0:T(8,128)(2,1)} %copy-done.72, ...), custom_call_target="tpu_custom_call" | custom-call | flops 19327352832 | bytes 37748736 | tf_op jit(solution)/shard_map/pallas_call | solution.py:266
  307.0 31.3 %shard_map.289 = (bf16[256,2048]{1,0:T(8,128)(2,1)}, bf16[256,2048]{1,0:T(8,128)(2,1)}, f32[256,128]{1,0:T(8,128)}, bf16[4,1024,768]{2,1,0:T(8,128)(2,1)}, bf16[...) custom-call(s32[2]{0:T(128)} %pad_add_fusion.4.half_ref, ...), custom_call_target="tpu_custom_call", output_to_operand_aliasing={{3}: (15, {}), {4}: (16, {}), {5}: (17, {})} | custom-call | flops 19327352832 | bytes 37748736 | tf_op jit(solution)/shard_map/pallas_call | solution.py:266
  340.5 31.3 %shard_map.290 = (bf16[256,2048]{1,0:T(8,128)(2,1)}, bf16[256,2048]{1,0:T(8,128)(2,1)}, f32[256,128]{1,0:T(8,128)}, bf16[4,1024,768]{2,1,0:T(8,128)(2,1)}, bf16[...) custom-call(s32[2]{0:T(128)} %pad_add_fusion.3.half_ref, ...), custom_call_target="tpu_custom_call", output_to_operand_aliasing={{3}: (16, {}), {4}: (17, {}), {5}: (18, {})} | custom-call | flops 19327352832 | bytes 37748736 | tf_op jit(solution)/shard_map/pallas_call | solution.py:266
  374.8 31.3 %shard_map.291 = (bf16[256,2048]{1,0:T(8,128)(2,1)}, bf16[256,2048]{1,0:T(8,128)(2,1)}, f32[256,128]{1,0:T(8,128)}, bf16[4,1024,768]{2,1,0:T(8,128)(2,1)}, bf16[...) custom-call(s32[2]{0:T(128)} %pad_add_fusion.2.half_ref, ...), custom_call_target="tpu_custom_call", output_to_operand_aliasing={{3}: (16, {}), {4}: (17, {}), {5}: (18, {})} | custom-call | flops 19327352832 | bytes 37748736 | tf_op jit(solution)/shard_map/pallas_call | solution.py:266
  436.5 9.4 %shard_map.294 = bf16[1024,2304]{1,0:T(8,128)(2,1)} custom-call(s32[1]{0:T(128)} %bitcast.7.core_ref.c, bf16[2048,1024]{1,0:T(8,128)(2,1)S(1)} %copy-done.2, bf16[2048,1024]{1,0:T(8,128)(2,1)} %bitcast.65, bf16[4,1024,1536]{2,1,0:T(8,128)(2,1)} %get-tuple-element.75.refs_2_, bf16[4,1024,768]{2,1,0:T(8,128)(2,1)} %get-tuple-element.76.refs_3_, ...), custom_call_target="tpu_custom_call" | custom-call | flops 4831838208 | bytes 8912896 | tf_op jit(solution)/shard_map/pallas_call | solution.py:330
  467.6 9.4 %shard_map.295 = bf16[1024,2304]{1,0:T(8,128)(2,1)} custom-call(s32[1]{0:T(128)} %bitcast.7.core_ref.c, bf16[2048,1024]{1,0:T(8,128)(2,1)S(1)} %copy-done.2, bf16[2048,1024]{1,0:T(8,128)(2,1)} %bitcast.66, bf16[4,1024,1536]{2,1,0:T(8,128)(2,1)} %get-tuple-element.75.refs_2_, bf16[4,1024,768]{2,1,0:T(8,128)(2,1)} %get-tuple-element.76.refs_3_, ...), custom_call_target="tpu_custom_call" | custom-call | flops 4831838208 | bytes 8912896 | tf_op jit(solution)/shard_map/pallas_call | solution.py:330
  494.2 10.2 %shard_map.296 = bf16[1024,2304]{1,0:T(8,128)(2,1)} custom-call(s32[1]{0:T(128)} %bitcast.7.core_ref.c, bf16[2048,1024]{1,0:T(8,128)(2,1)S(1)} %copy-done.3, bf16[2048,1024]{1,0:T(8,128)(2,1)} %bitcast.67, bf16[4,1024,1536]{2,1,0:T(8,128)(2,1)} %get-tuple-element.75.refs_2_, bf16[4,1024,768]{2,1,0:T(8,128)(2,1)} %get-tuple-element.76.refs_3_, ...), custom_call_target="tpu_custom_call" | custom-call | flops 4831838208 | bytes 8912896 | tf_op jit(solution)/shard_map/pallas_call | solution.py:330
  515.5 10.2 %shard_map.297 = bf16[1024,2304]{1,0:T(8,128)(2,1)} custom-call(s32[1]{0:T(128)} %bitcast.7.core_ref.c, bf16[2048,1024]{1,0:T(8,128)(2,1)S(1)} %copy-done.3, bf16[2048,1024]{1,0:T(8,128)(2,1)} %bitcast.68, bf16[4,1024,1536]{2,1,0:T(8,128)(2,1)} %get-tuple-element.75.refs_2_, bf16[4,1024,768]{2,1,0:T(8,128)(2,1)} %get-tuple-element.76.refs_3_, ...), custom_call_target="tpu_custom_call" | custom-call | flops 4831838208 | bytes 8912896 | tf_op jit(solution)/shard_map/pallas_call | solution.py:330
  527.8 31.9 %shard_map.298 = (bf16[1024,1024]{1,0:T(8,128)(2,1)S(1)}, f32[2048,128]{1,0:T(8,128)S(1)}, f32[2048,128]{1,0:T(8,128)S(1)}, f32[1,128]{1,0:T(1,128)S(1)}) custom-call(s32[5]{0:T(128)S(1)} %copy-done.21, bf16[8,1024,128]{2,1,0:T(8,128)(2,1)S(1)} %copy-done.28, bf16[2048,128]{1,0:T(8,128)(2,1)S(1)} %copy-done.15, bf16[128,2048]{1,0:T(8,128)(2,1)S(1)} %copy.122.kt_ref, ...), custom_call_target="tpu_custom_call" | custom-call | flops 21474836480 | bytes 12582912 | tf_op jit(solution)/shard_map/pallas_call | solution.py:489
  568.7 12.0 %collective-permute-start.29 = (bf16[1024,256]{1,0:T(8,128)(2,1)S(1)}, bf16[1024,256]{1,0:T(8,128)(2,1)S(1)}, u32[]{:S(2)}, u32[]{:S(2)}) collective-permute-start(bf16[1024,256]{1,0:T(8,128)(2,1)S(1)} %pad_maximum_fusion.13), channel_id=1, source_target_pairs={{0,4},{4,0},{1,5},{5,1},{2,6},{6,2},{3,7},{7,3},{8,12},{12,8},{9,1... | collective-permute-start | bytes 1572872 | tf_op jit(solution)/shard_map/ppermute | solution.py:66
  584.1 10.4 %shard_map.300 = bf16[1024,2304]{1,0:T(8,128)(2,1)} custom-call(s32[1]{0:T(128)} %bitcast.7.core_ref.c, bf16[2048,1024]{1,0:T(8,128)(2,1)S(1)} %copy-done.4, bf16[2048,1024]{1,0:T(8,128)(2,1)} %bitcast.69, bf16[4,1024,1536]{2,1,0:T(8,128)(2,1)} %get-tuple-element.75.refs_2_, bf16[4,1024,768]{2,1,0:T(8,128)(2,1)} %get-tuple-element.76.refs_3_, ...), custom_call_target="tpu_custom_call" | custom-call | flops 4831838208 | bytes 8912896 | tf_op jit(solution)/shard_map/pallas_call | solution.py:330
  622.4 10.1 %shard_map.301.a = bf16[1024,2304]{1,0:T(8,128)(2,1)} custom-call(s32[1]{0:T(128)} %bitcast.7.core_ref.c, bf16[2048,1024]{1,0:T(8,128)(2,1)S(1)} %copy-done.4, bf16[2048,1024]{1,0:T(8,128)(2,1)} %bitcast.70, bf16[4,1024,1536]{2,1,0:T(8,128)(2,1)} %get-tuple-element.75.refs_2_, bf16[4,1024,768]{2,1,0:T(8,128)(2,1)} %get-tuple-element.76.refs_3_, ...), custom_call_target="tpu_custom_call" | custom-call | flops 4831838208 | bytes 8912896 | tf_op jit(solution)/shard_map/pallas_call | solution.py:330
  641.7 10.3 %shard_map.307 = bf16[1024,2304]{1,0:T(8,128)(2,1)} custom-call(s32[1]{0:T(128)} %bitcast.7.core_ref.c, bf16[2048,1024]{1,0:T(8,128)(2,1)S(1)} %copy-done.5, bf16[2048,1024]{1,0:T(8,128)(2,1)} %bitcast.71, bf16[4,1024,1536]{2,1,0:T(8,128)(2,1)} %get-tuple-element.75.refs_2_, bf16[4,1024,768]{2,1,0:T(8,128)(2,1)} %get-tuple-element.76.refs_3_, ...), custom_call_target="tpu_custom_call" | custom-call | flops 4831838208 | bytes 8912896 | tf_op jit(solution)/shard_map/pallas_call | solution.py:330
  654.8 62.8 %collective-permute-done.32 = bf16[256,2048]{1,0:T(8,128)(2,1)S(1)} collective-permute-done((bf16[256,2048]{1,0:T(8,128)(2,1)S(1)}, bf16[256,2048]{1,0:T(8,128)(2,1)S(1)}, u32[]{:S(2)}, u32[]{:S(2)}) %collective-permute-start.32) | collective-permute-done | bytes 1048608 | tf_op jit(solution)/shard_map/ppermute | solution.py:96
  732.6 73.0 %all-reduce.4.cloned.1.call-done = (bf16[1024,1024]{1,0:T(8,128)(2,1)}, bf16[1024,256]{1,0:T(8,128)(2,1)}, bf16[512,2048]{1,0:T(8,128)(2,1)}) async-done(((bf16[1024,1024]{1,0:T(8,128)(2,1)}, bf16[1024,256]{1,0:T(8,128)(2,1)}, bf16[512,2048]{1,0:T(8,128)(2,1)}), (bf16[1024,1024]{1,0:T(8,128)(2,1)}, bf16[1024,256]{1,0:T(8,128)(2,1)}, bf16[512,2048]{1,0:T(8,128)(2,1)})) %all-reduce.4.cloned.1.call-update) | async-done | bytes 4718608 | tf_op jit(solution)/shard_map/psum | solution.py:877
  822.3 10.1 %shard_map.308.a = bf16[1024,2304]{1,0:T(8,128)(2,1)} custom-call(s32[1]{0:T(128)} %bitcast.7.core_ref.c, bf16[2048,1024]{1,0:T(8,128)(2,1)S(1)} %copy-done.6, bf16[2048,1024]{1,0:T(8,128)(2,1)} %bitcast.72, bf16[4,1024,1536]{2,1,0:T(8,128)(2,1)} %get-tuple-element.75.refs_2_, bf16[4,1024,768]{2,1,0:T(8,128)(2,1)} %get-tuple-element.76.refs_3_, ...), custom_call_target="tpu_custom_call" | custom-call | flops 4831838208 | bytes 8912896 | tf_op jit(solution)/shard_map/pallas_call | solution.py:330
  832.4 9.6 %collective-permute-done.50 = bf16[1024,256]{1,0:T(8,128)(2,1)S(1)} collective-permute-done((bf16[1024,256]{1,0:T(8,128)(2,1)S(1)}, bf16[1024,256]{1,0:T(8,128)(2,1)S(1)}, u32[]{:S(2)}, u32[]{:S(2)}) %collective-permute-start.50) | collective-permute-done | bytes 524320 | tf_op jit(solution)/shard_map/ppermute | solution.py:96
  (538 shorter events, 385.1 us)
Async XLA Ops:
  7.2 798.4 %all-reduce.4.cloned.1.call-start = ((), (), s32[]{:S(2)}) async-start(), calls=%async_computation | async-start | bytes 9437184 | tf_op jit(solution)/shard_map/psum | solution.py:877
  7.3 72.3 %collective-permute-start.2 = (bf16[2048,1536]{1,0:T(8,128)(2,1)}, bf16[2048,1536]{1,0:T(8,128)(2,1)}, u32[]{:S(2)}, u32[]{:S(2)}) collective-permute-start(bf16[2048,1536]{1,0:T(8,128)(2,1)} %bitcast.79), channel_id=1, source_target_pairs={{0,8},{4,20},{8,0},{12,28},{16,24},{20,4},{24,16},{28,12},{1,9},{5... | collective-permute-start | bytes 18874376 | tf_op jit(solution)/shard_map/ppermute | solution.py:96
  25.8 90.1 %collective-permute-start.3 = (bf16[768,2048]{1,0:T(8,128)(2,1)}, bf16[768,2048]{1,0:T(8,128)(2,1)}, u32[]{:S(2)}, u32[]{:S(2)}) collective-permute-start(bf16[768,2048]{1,0:T(8,128)(2,1)} %bitcast.84), channel_id=1, source_target_pairs={{0,8},{4,20},{8,0},{12,28},{16,24},{20,4},{24,16},{28,12},{1,9},{5... | collective-permute-start | bytes 9437192 | tf_op jit(solution)/shard_map/ppermute | solution.py:96
  80.8 92.9 %collective-permute-start.9 = (bf16[2048,1536]{1,0:T(8,128)(2,1)}, bf16[2048,1536]{1,0:T(8,128)(2,1)}, u32[]{:S(2)}, u32[]{:S(2)}) collective-permute-start(bf16[2048,1536]{1,0:T(8,128)(2,1)} %shard_map.285.refs_6_), channel_id=1, source_target_pairs={{0,4},{4,0},{1,5},{5,1},{2,6},{6,2},{3,7},{7,3},{8,12},{12,8},{9,1... | collective-permute-start | bytes 18874376 | tf_op jit(solution)/shard_map/ppermute | solution.py:146
  153.8 55.7 %collective-permute-start.10 = (bf16[768,2048]{1,0:T(8,128)(2,1)}, bf16[768,2048]{1,0:T(8,128)(2,1)}, u32[]{:S(2)}, u32[]{:S(2)}) collective-permute-start(bf16[768,2048]{1,0:T(8,128)(2,1)} %collective-permute-done.3.refs_7_), channel_id=1, source_target_pairs={{0,4},{4,0},{1,5},{5,1},{2,6},{6,2},{3,7},{7,3},{8,12},{12,8},{9,1... | collective-permute-start | bytes 9437192 | tf_op jit(solution)/shard_map/ppermute | solution.py:146
  177.5 37.6 %collective-permute-start.11 = (bf16[1024,1536]{1,0:T(8,128)(2,1)}, bf16[1024,1536]{1,0:T(8,128)(2,1)}, u32[]{:S(2)}, u32[]{:S(2)}) collective-permute-start(bf16[1024,1536]{1,0:T(8,128)(2,1)} %constant_dynamic-slice_fusion.8), channel_id=1, source_target_pairs={{0,8},{4,20},{8,0},{12,28},{16,24},{20,4},{24,16},{28,12},{1,9},{5... | collective-permute-start | bytes 9437192 | tf_op jit(solution)/shard_map/ppermute | solution.py:96
  215.1 60.3 %collective-permute-start.13 = (bf16[1024,1536]{1,0:T(8,128)(2,1)}, bf16[1024,1536]{1,0:T(8,128)(2,1)}, u32[]{:S(2)}, u32[]{:S(2)}) collective-permute-start(bf16[1024,1536]{1,0:T(8,128)(2,1)} %collective-permute-done.11.refs_10_), channel_id=1, source_target_pairs={{0,4},{4,0},{1,5},{5,1},{2,6},{6,2},{3,7},{7,3},{8,12},{12,8},{9,1... | collective-permute-start | bytes 9437192 | tf_op jit(solution)/shard_map/ppermute | solution.py:146
  445.9 45.8 %collective-permute-start.27 = (bf16[1024,2304]{1,0:T(8,128)(2,1)}, bf16[1024,2304]{1,0:T(8,128)(2,1)}, u32[]{:S(2)}, u32[]{:S(2)}) collective-permute-start(bf16[1024,2304]{1,0:T(8,128)(2,1)} %shard_map.294), channel_id=1, source_target_pairs={{0,4},{4,0},{1,5},{5,1},{2,6},{6,2},{3,7},{7,3},{8,12},{12,8},{9,1... | collective-permute-start | bytes 14155784 | tf_op jit(solution)/shard_map/ppermute | solution.py:146
  477.0 38.5 %collective-permute-start.26 = (bf16[1024,2304]{1,0:T(8,128)(2,1)}, bf16[1024,2304]{1,0:T(8,128)(2,1)}, u32[]{:S(2)}, u32[]{:S(2)}) collective-permute-start(bf16[1024,2304]{1,0:T(8,128)(2,1)} %shard_map.295), channel_id=1, source_target_pairs={{0,4},{4,0},{1,5},{5,1},{2,6},{6,2},{3,7},{7,3},{8,12},{12,8},{9,1... | collective-permute-start | bytes 14155784 | tf_op jit(solution)/shard_map/ppermute | solution.py:146
  491.4 119.1 %collective-permute-start.53 = (bf16[512,2048]{1,0:T(8,128)(2,1)}, bf16[512,2048]{1,0:T(8,128)(2,1)}, u32[]{:S(2)}, u32[]{:S(2)}) collective-permute-start(bf16[512,2048]{1,0:T(8,128)(2,1)} %constant_dynamic-slice_fusion), channel_id=1, source_target_pairs={{0,4},{4,0},{1,5},{5,1},{2,6},{6,2},{3,7},{7,3},{8,12},{12,8},{9,1... | collective-permute-start | bytes 6291464 | tf_op jit(solution)/shard_map/ppermute | solution.py:146
  504.4 61.5 %collective-permute-start.28 = (bf16[1024,2304]{1,0:T(8,128)(2,1)}, bf16[1024,2304]{1,0:T(8,128)(2,1)}, u32[]{:S(2)}, u32[]{:S(2)}) collective-permute-start(bf16[1024,2304]{1,0:T(8,128)(2,1)} %shard_map.296), channel_id=1, source_target_pairs={{0,8},{4,20},{8,0},{12,28},{16,24},{20,4},{24,16},{28,12},{1,9},{5... | collective-permute-start | bytes 14155784 | tf_op jit(solution)/shard_map/ppermute | solution.py:96
  526.5 96.0 %collective-permute-start.31 = (bf16[1024,2304]{1,0:T(8,128)(2,1)}, bf16[1024,2304]{1,0:T(8,128)(2,1)}, u32[]{:S(2)}, u32[]{:S(2)}) collective-permute-start(bf16[1024,2304]{1,0:T(8,128)(2,1)} %shard_map.297), channel_id=1, source_target_pairs={{0,8},{4,20},{8,0},{12,28},{16,24},{20,4},{24,16},{28,12},{1,9},{5... | collective-permute-start | bytes 14155784 | tf_op jit(solution)/shard_map/ppermute | solution.py:96
  582.2 35.7 %collective-permute-start.46 = (bf16[1024,1024]{1,0:T(8,128)(2,1)}, bf16[1024,1024]{1,0:T(8,128)(2,1)}, u32[]{:S(2)}, u32[]{:S(2)}) collective-permute-start(bf16[1024,1024]{1,0:T(8,128)(2,1)} %constant_dynamic-slice_fusion.2), channel_id=1, source_target_pairs={{0,4},{4,0},{1,5},{5,1},{2,6},{6,2},{3,7},{7,3},{8,12},{12,8},{9,1... | collective-permute-start | bytes 6291464 | tf_op jit(solution)/shard_map/ppermute | solution.py:146
  594.5 45.0 %collective-permute-start.39 = (bf16[1024,2304]{1,0:T(8,128)(2,1)}, bf16[1024,2304]{1,0:T(8,128)(2,1)}, u32[]{:S(2)}, u32[]{:S(2)}) collective-permute-start(bf16[1024,2304]{1,0:T(8,128)(2,1)} %shard_map.300), channel_id=1, source_target_pairs={{0,4},{4,0},{1,5},{5,1},{2,6},{6,2},{3,7},{7,3},{8,12},{12,8},{9,1... | collective-permute-start | bytes 14155784 | tf_op jit(solution)/shard_map/ppermute | solution.py:146
  652.0 170.2 %collective-permute-start.40 = (bf16[1024,2304]{1,0:T(8,128)(2,1)}, bf16[1024,2304]{1,0:T(8,128)(2,1)}, u32[]{:S(2)}, u32[]{:S(2)}) collective-permute-start(bf16[1024,2304]{1,0:T(8,128)(2,1)} %shard_map.307), channel_id=1, source_target_pairs={{0,8},{4,20},{8,0},{12,28},{16,24},{20,4},{24,16},{28,12},{1,9},{5... | collective-permute-start | bytes 14155784 | tf_op jit(solution)/shard_map/ppermute | solution.py:96
  653.0 64.6 %collective-permute-start.32 = (bf16[256,2048]{1,0:T(8,128)(2,1)S(1)}, bf16[256,2048]{1,0:T(8,128)(2,1)S(1)}, u32[]{:S(2)}, u32[]{:S(2)}) collective-permute-start(bf16[256,2048]{1,0:T(8,128)(2,1)S(1)} %copy-done.45), channel_id=1, source_target_pairs={{0,8},{4,20},{8,0},{12,28},{16,24},{20,4},{24,16},{28,12},{1,9},{5... | collective-permute-start | bytes 3145736 | tf_op jit(solution)/shard_map/ppermute | solution.py:96
  724.2 83.5 %collective-permute-start.36 = (bf16[256,2048]{1,0:T(8,128)(2,1)}, bf16[256,2048]{1,0:T(8,128)(2,1)}, u32[]{:S(2)}, u32[]{:S(2)}) collective-permute-start(bf16[256,2048]{1,0:T(8,128)(2,1)} %fusion.19.refs_0_), channel_id=1, source_target_pairs={{0,8},{4,20},{8,0},{12,28},{16,24},{20,4},{24,16},{28,12},{1,9},{5... | collective-permute-start | bytes 3145736 | tf_op jit(solution)/shard_map/ppermute | solution.py:96
  728.4 86.4 %collective-permute-start.37 = (bf16[256,2048]{1,0:T(8,128)(2,1)}, bf16[256,2048]{1,0:T(8,128)(2,1)}, u32[]{:S(2)}, u32[]{:S(2)}) collective-permute-start(bf16[256,2048]{1,0:T(8,128)(2,1)} %fusion.19.refs_0_), channel_id=1, source_target_pairs={{0,16},{4,12},{8,24},{12,4},{16,0},{20,28},{24,8},{28,20},{1,17},{... | collective-permute-start | bytes 3145736 | tf_op jit(solution)/shard_map/ppermute | solution.py:96
  730.3 85.2 %collective-permute-start.33 = (bf16[256,2048]{1,0:T(8,128)(2,1)}, bf16[256,2048]{1,0:T(8,128)(2,1)S(1)}, u32[]{:S(2)}, u32[]{:S(2)}) collective-permute-start(bf16[256,2048]{1,0:T(8,128)(2,1)} %shard_map.303.refs_0_), channel_id=1, source_target_pairs={{0,8},{4,20},{8,0},{12,28},{16,24},{20,4},{24,16},{28,12},{1,9},{5... | collective-permute-start | bytes 3145736 | tf_op jit(solution)/shard_map/ppermute | solution.py:96
  815.5 62.9 %collective-permute-start.54 = (bf16[512,2048]{1,0:T(8,128)(2,1)S(1)}, bf16[512,2048]{1,0:T(8,128)(2,1)}, u32[]{:S(2)}, u32[]{:S(2)}) collective-permute-start(bf16[512,2048]{1,0:T(8,128)(2,1)S(1)} %copy-done.66), channel_id=1, source_target_pairs={{0,4},{4,0},{1,5},{5,1},{2,6},{6,2},{3,7},{7,3},{8,12},{12,8},{9,1... | collective-permute-start | bytes 6291464 | tf_op jit(solution)/shard_map/ppermute | solution.py:146
  832.3 94.1 %collective-permute-start.55 = (bf16[1024,2304]{1,0:T(8,128)(2,1)}, bf16[1024,2304]{1,0:T(8,128)(2,1)}, u32[]{:S(2)}, u32[]{:S(2)}) collective-permute-start(bf16[1024,2304]{1,0:T(8,128)(2,1)} %shard_map.301.a), channel_id=1, source_target_pairs={{0,4},{4,0},{1,5},{5,1},{2,6},{6,2},{3,7},{7,3},{8,12},{12,8},{9,1... | collective-permute-start | bytes 14155784 | tf_op jit(solution)/shard_map/ppermute | solution.py:146
  842.0 76.4 %collective-permute-start.56 = (bf16[1024,2304]{1,0:T(8,128)(2,1)}, bf16[1024,2304]{1,0:T(8,128)(2,1)}, u32[]{:S(2)}, u32[]{:S(2)}) collective-permute-start(bf16[1024,2304]{1,0:T(8,128)(2,1)} %shard_map.308.a), channel_id=1, source_target_pairs={{0,4},{4,0},{1,5},{5,1},{2,6},{6,2},{3,7},{7,3},{8,12},{12,8},{9,1... | collective-permute-start | bytes 14155784 | tf_op jit(solution)/shard_map/ppermute | solution.py:146
  849.8 41.2 %collective-permute-start.47 = (bf16[1024,1024]{1,0:T(8,128)(2,1)}, bf16[1024,1024]{1,0:T(8,128)(2,1)}, u32[]{:S(2)}, u32[]{:S(2)}) collective-permute-start(bf16[1024,1024]{1,0:T(8,128)(2,1)} %get-tuple-element.163), channel_id=1, source_target_pairs={{0,4},{4,0},{1,5},{5,1},{2,6},{6,2},{3,7},{7,3},{8,12},{12,8},{9,1... | collective-permute-start | bytes 6291464 | tf_op jit(solution)/shard_map/ppermute | solution.py:146
  862.4 39.6 %collective-permute-start.52 = (bf16[1024,1024]{1,0:T(8,128)(2,1)}, bf16[1024,1024]{1,0:T(8,128)(2,1)}, u32[]{:S(2)}, u32[]{:S(2)}) collective-permute-start(bf16[1024,1024]{1,0:T(8,128)(2,1)} %dynamic-slice_dynamic-update-slice_fusion), channel_id=1, source_target_pairs={{0,4},{4,0},{1,5},{5,1},{2,6},{6,2},{3,7},{7,3},{8,12},{12,8},{9,1... | collective-permute-start | bytes 6291464 | tf_op jit(solution)/shard_map/ppermute | solution.py:146
  (142 other events, 2815.3 us)
Sparse Core Ops, SparseCore 0:
  634.9 170.6 all-reduce.3
